TPU v7x, 256 devices: a whole 4x4x8 slice. The times are simulated.
256 devices in a mesh: wide: 32 (over z, x), narrow: 8 (over y, core).
Axes of the slice: x: 4, y: 4, z: 8, core: 2. Of those that a mesh axis runs over, the one named last changes fastest.
Arguments:
- table: float32 [65536, 512], P('wide'), may hold values from -6 to 6
- accum: float32 [65536], P('wide'), may hold values from 0.1 to 4
- ids: int32 [32, 2048], P('wide', 'narrow'), may hold values from 0 to 65535, as said below
- lengths: int32 [32], P('wide'), may hold values from 1 to 2048, 40960 in all
- w_uvqk: bfloat16 [512, 2048], replicated, may hold values from -0.25 to 0.25
- w_out: bfloat16 [512, 512], replicated, may hold values from -0.25 to 0.25
- cotangent: bfloat16 [32, 2048, 512], P('wide', 'narrow'), may hold values from -6 to 6
Outputs:
- output: bfloat16 [32, 2048, 512], P('wide', 'narrow')
- new_table: float32 [65536, 512], P('wide')
- new_accum: float32 [65536], P('wide')
Inputs may be any that keep to these rules, and one draw needn't show every extreme that they name: Row r belongs to owner r // 2048. Among the 256 slots that one device holds (aligned blocks by both axes), at most 16 ids belong to any one owner, and in every draw one owner gets exactly 16 from every device. Ids at slots past a sequence's length are present but unused. The lengths sum to 40960; the longest is exactly 2048.
All inputs are finite; a program needn't handle non-finite values. No bound on the sum of `lengths` on one device may be relied on, other than what follows from the above.
Results may differ from a plain program's by a relative error of at most 0.007.
Values may be sent and summed in bfloat16 or wider, within the bound.
A program may use at most 128 MiB of HBM per device.

v0:
```python
import math

import jax
import jax.numpy as jnp
from jax import lax
from jax.sharding import PartitionSpec as P

HEADS = 8
HD = 64


norm_eps = 1e-05
learning_rate = 0.5


def silu_slope(value):
    sigma = jax.nn.sigmoid(value)
    return sigma * (1.0 + value * (1.0 - sigma))


def layer_norm(value):
    center = value - jnp.mean(value, axis=-1, keepdims=True)
    inverse = lax.rsqrt(jnp.mean(center * center, axis=-1, keepdims=True) + norm_eps)
    return (center * inverse, inverse)


def norm_backward(grad, normed, inverse):
    return inverse * (
        grad
        - jnp.mean(grad, axis=-1, keepdims=True)
        - normed * jnp.mean(grad * normed, axis=-1, keepdims=True)
    )


def adagrad_rows(rows_now, accum_now, grads):
    accum_next = accum_now + jnp.mean(grads * grads, axis=1)
    return (rows_now - learning_rate * grads / jnp.sqrt(accum_next)[:, None], accum_next)


def local(table, accum, ids, lengths, w_uvqk, w_out, cotangent):
    n_wide = lax.axis_size("wide")
    seq_count, stretch = ids.shape
    tokens = seq_count * stretch
    rows_dev, width = table.shape
    att = HEADS * HD
    capacity = max(2, 2 * tokens // n_wide)
    flat_ids = ids.reshape(tokens)
    owner_id = flat_ids // rows_dev
    local_row = flat_ids % rows_dev
    owner_hits = (owner_id[:, None] == jnp.arange(n_wide, dtype=jnp.int32)[None, :]).astype(
        jnp.int32
    )
    earlier = jnp.cumsum(owner_hits, axis=0) - owner_hits
    slot_index = jnp.sum(earlier * owner_hits, axis=1)
    target = owner_id * capacity + slot_index
    requests = (
        jnp.zeros((n_wide * capacity,), jnp.int32)
        .at[target]
        .set(local_row)
        .reshape(n_wide, capacity)
    )
    incoming = lax.all_to_all(requests, "wide", split_axis=0, concat_axis=0, tiled=True)
    count = incoming.shape[1]
    fetched = table[incoming.reshape(-1)].astype(jnp.bfloat16).reshape(n_wide, count, width)
    replies = lax.all_to_all(fetched, "wide", split_axis=0, concat_axis=0, tiled=True)
    replies, received = (replies, incoming)
    embed = replies.reshape(n_wide * capacity, width)[target]
    positions = lax.axis_index("narrow") * stretch + jnp.arange(stretch, dtype=jnp.int32)
    live = (positions[None, :] < lengths[:, None]).reshape(tokens)
    embed_f = embed.astype(jnp.float32)
    normed1, inverse1 = layer_norm(embed_f)
    hidden = jnp.dot(normed1.astype(jnp.bfloat16), w_uvqk, preferred_element_type=jnp.float32)
    hidden_u = hidden[:, :att]
    hidden_rest = hidden[:, att:].reshape(tokens, HEADS, 3, HD)
    part_index = jnp.arange(3, dtype=jnp.int32)[None, None, :, None]
    act_u = jax.nn.silu(hidden_u).astype(jnp.bfloat16)
    act_rest = jnp.where(part_index == 0, hidden_rest, jax.nn.silu(hidden_rest)).astype(
        jnp.bfloat16
    )
    by_head = lax.all_to_all(
        act_rest.reshape(seq_count, stretch, HEADS, 3 * HD),
        "narrow",
        split_axis=2,
        concat_axis=1,
        tiled=True,
    )
    full_len = by_head.shape[1]
    values = by_head[..., :HD]
    queries = by_head[..., HD : 2 * HD]
    keys_all = by_head[..., 2 * HD :]
    scale = 1.0 / math.sqrt(HD)
    block = min(512, full_len)
    key_pos = jnp.arange(full_len, dtype=jnp.int32)

    def block_scores(start):
        return (
            jnp.einsum(
                "sbhd,skhd->shbk",
                queries[:, start : start + block],
                keys_all,
                preferred_element_type=jnp.float32,
            )
            * scale
        )

    def block_mask(start):
        rows = start + jnp.arange(block, dtype=jnp.int32)
        return (key_pos[None, None, None, :] <= rows[None, None, :, None]) & (
            rows[None, None, :, None] < lengths[:, None, None, None]
        )

    pieces = []
    for start in range(0, full_len, block):
        scores = block_scores(start)
        weights = jnp.where(block_mask(start), jax.nn.silu(scores), 0.0).astype(jnp.bfloat16)
        pieces.append(
            jnp.einsum(
                "shbk,skhd->sbhd", weights, values, preferred_element_type=jnp.float32
            ).astype(jnp.bfloat16)
        )
    attended = jnp.concatenate(pieces, axis=1)
    merged_heads = lax.all_to_all(
        attended, "narrow", split_axis=1, concat_axis=2, tiled=True
    ).reshape(tokens, att)
    normed2, inverse2 = layer_norm(merged_heads.astype(jnp.float32))
    act_u_f = act_u.astype(jnp.float32)
    mixed = (normed2 * act_u_f).astype(jnp.bfloat16)
    result = embed_f + jnp.dot(mixed, w_out, preferred_element_type=jnp.float32)
    output = (
        jnp.where(live[:, None], result, 0.0)
        .astype(jnp.bfloat16)
        .reshape(seq_count, stretch, width)
    )
    upstream = jnp.where(
        live[:, None], cotangent.reshape(tokens, width), jnp.zeros((), jnp.bfloat16)
    )
    grad_mixed = lax.dot_general(
        upstream, w_out, (((1,), (1,)), ((), ())), preferred_element_type=jnp.float32
    )
    grad_norm2 = grad_mixed * act_u_f
    grad_u = grad_mixed * normed2
    grad_attended = (
        norm_backward(grad_norm2, normed2, inverse2)
        .astype(jnp.bfloat16)
        .reshape(seq_count, stretch, HEADS, HD)
    )
    grad_out = lax.all_to_all(grad_attended, "narrow", split_axis=2, concat_axis=1, tiled=True)
    grad_values = jnp.zeros(values.shape, jnp.float32)
    grad_keys = jnp.zeros(keys_all.shape, jnp.float32)
    query_pieces = []
    for index, start in enumerate(range(0, full_len, block)):
        scores = block_scores(start)
        mask = block_mask(start)
        weights = jnp.where(mask, jax.nn.silu(scores), 0.0).astype(jnp.bfloat16)
        grad_block = grad_out[:, start : start + block]
        grad_weights = jnp.einsum(
            "sbhd,skhd->shbk", grad_block, values, preferred_element_type=jnp.float32
        )
        grad_scores = jnp.where(mask, grad_weights * silu_slope(scores), 0.0).astype(jnp.bfloat16)
        grad_values = grad_values + jnp.einsum(
            "shbk,sbhd->skhd", weights, grad_block, preferred_element_type=jnp.float32
        )
        query_pieces.append(
            jnp.einsum("shbk,skhd->sbhd", grad_scores, keys_all, preferred_element_type=jnp.float32)
            * scale
        )
        grad_keys = (
            grad_keys
            + jnp.einsum(
                "shbk,sbhd->skhd",
                grad_scores,
                queries[:, start : start + block],
                preferred_element_type=jnp.float32,
            )
            * scale
        )
    grad_queries = jnp.concatenate(query_pieces, axis=1)
    grad_packed = jnp.concatenate(
        [
            grad_values.astype(jnp.bfloat16),
            grad_queries.astype(jnp.bfloat16),
            grad_keys.astype(jnp.bfloat16),
        ],
        axis=-1,
    )
    returned = (
        lax.all_to_all(grad_packed, "narrow", split_axis=1, concat_axis=2, tiled=True)
        .reshape(tokens, HEADS, 3, HD)
        .astype(jnp.float32)
    )
    grad_rest = jnp.where(part_index == 0, returned, returned * silu_slope(hidden_rest)).reshape(
        tokens, 3 * att
    )
    grad_hidden = jnp.concatenate([grad_u * silu_slope(hidden_u), grad_rest], axis=1).astype(
        jnp.bfloat16
    )
    grad_norm1 = lax.dot_general(
        grad_hidden, w_uvqk, (((1,), (1,)), ((), ())), preferred_element_type=jnp.float32
    )
    grad_embed = jnp.where(
        live[:, None],
        norm_backward(grad_norm1, normed1, inverse1) + upstream.astype(jnp.float32),
        0.0,
    )
    outgoing = (
        jnp.zeros((n_wide * capacity, width), jnp.float32)
        .at[target]
        .set(grad_embed)
        .reshape(n_wide, capacity, width)
    )
    arriving = lax.all_to_all(
        outgoing.astype(jnp.bfloat16), "wide", split_axis=0, concat_axis=0, tiled=True
    ).astype(outgoing.dtype)
    row_grads = (
        jnp.zeros((rows_dev, width), jnp.float32)
        .at[received.reshape(-1)]
        .add(arriving.reshape(-1, width))
    )
    summed = lax.psum(row_grads.astype(jnp.bfloat16), "narrow").astype(jnp.float32)
    new_table, new_accum = adagrad_rows(table, accum, summed)
    return (output, new_table, new_accum)


def solution(mesh):
    in_specs = (
        P("wide", None),
        P("wide"),
        P("wide", "narrow"),
        P("wide"),
        P(),
        P(),
        P("wide", "narrow", None),
    )
    out_specs = (P("wide", "narrow", None), P("wide", None), P("wide"))
    return jax.shard_map(local, mesh=mesh, in_specs=in_specs, out_specs=out_specs, check_vma=False)
```

profile of v0, /device:TPU:1, one launch (start us, length us, event | category | flops | bytes accessed | tf_op | source)
XLA Modules:
  0.0 372.7 jit_solution(17870003144151056957)
XLA Ops:
  11.8 20.2 %all_to_all.73 = s32[32,1,16]{2,1,0:T(1,128)S(1)} all-to-all(s32[32,1,16]{2,1,0:T(1,128)S(1)} %bitcast.261), channel_id=1, replica_groups=mesh['wide'=32,'narrow'=8] {'wide'}, dimensions={0} | all-to-all | bytes 4096 | tf_op jit(solution)/shard_map/all_to_all | solution.py:62
  33.4 4.8 %gather_fusion = bf16[512,512]{1,0:T(8,128)(2,1)} fusion(f32[2048,512]{1,0:T(8,128)} %param.7, s32[1024]{0:T(1024)S(1)} %pad_clamp_fusion.1), kind=kCustom, calls=%fused_computation | custom fusion | bytes 1050624 | tf_op jit(solution)/shard_map/gather | solution.py:64
  38.2 3.9 %all-to-all-start.1 = ((bf16[32,16,512]{2,1,0:T(8,128)(2,1)}), bf16[32,16,512]{2,1,0:T(8,128)(2,1)S(1)}, u32[]{:S(2)}, u32[]{:S(2)}) async-start(bf16[32,16,512]{2,1,0:T(8,128)(2,1)} %bitcast.9), calls=%async_computation.1 | async-start | bytes 1048576 | tf_op jit(solution)/shard_map/all_to_all | solution.py:65
  42.3 14.5 %all-to-all-done.1 = bf16[32,16,512]{2,1,0:T(8,128)(2,1)S(1)} async-done(((bf16[32,16,512]{2,1,0:T(8,128)(2,1)}), bf16[32,16,512]{2,1,0:T(8,128)(2,1)S(1)}, u32[]{:S(2)}, u32[]{:S(2)}) %all-to-all-start.1) | async-done | bytes 524320 | tf_op jit(solution)/shard_map/all_to_all | solution.py:65
  61.7 3.0 copy.71
  67.5 9.2 %all-to-all-start.2 = ((bf16[1,256,8,192]{1,3,0,2:T(8,128)(2,1)}), bf16[1,256,8,192]{1,3,0,2:T(8,128)(2,1)S(1)}, u32[]{:S(2)}, u32[]{:S(2)}) async-start(bf16[1,256,8,192]{1,3,0,2:T(8,128)(2,1)} %fusion.36), calls=%async_computation.2 | async-start | bytes 1572864 | tf_op jit(solution)/shard_map/all_to_all | solution.py:80
  77.4 11.5 %all-to-all-done.2 = bf16[1,256,8,192]{1,3,0,2:T(8,128)(2,1)S(1)} async-done(((bf16[1,256,8,192]{1,3,0,2:T(8,128)(2,1)}), bf16[1,256,8,192]{1,3,0,2:T(8,128)(2,1)S(1)}, u32[]{:S(2)}, u32[]{:S(2)}) %all-to-all-start.2) | async-done | bytes 786464 | tf_op jit(solution)/shard_map/all_to_all | solution.py:80
  91.0 3.5 select_convert_fusion.6
  95.3 3.6 select_convert_fusion.7
  99.7 3.6 select_convert_fusion.5
  104.1 3.6 select_convert_fusion.4
  112.2 13.5 %reduce.12 = bf16[2048,64]{1,0:T(8,128)(2,1)} reduce(bf16[2048,1,1,64]{3,2,1,0:T(2,128)(2,1)} %bitcast.245, bf16[]{:T(256)} %broadcast.501), dimensions={1,2}, to_apply=%bitcast.169.reduce_sub_computation | reduce | bytes 524290
  127.9 4.5 %all-to-all-start.3 = ((bf16[8,2,8192]{2,1,0:T(2,128)(2,1)}), bf16[8,2,8192]{2,1,0:T(2,128)(2,1)S(1)}, u32[]{:S(2)}, u32[]{:S(2)}) async-start(bf16[8,2,8192]{2,1,0:T(2,128)(2,1)} %reshape.703), calls=%async_computation.3 | async-start | bytes 524288 | tf_op jit(solution)/shard_map/all_to_all | solution.py:122
  132.4 6.5 %all-to-all-done.3 = bf16[8,2,8192]{2,1,0:T(2,128)(2,1)S(1)} async-done(((bf16[8,2,8192]{2,1,0:T(2,128)(2,1)}), bf16[8,2,8192]{2,1,0:T(2,128)(2,1)S(1)}, u32[]{:S(2)}, u32[]{:S(2)}) %all-to-all-start.3) | async-done | bytes 262176 | tf_op jit(solution)/shard_map/all_to_all | solution.py:122
  140.7 3.0 bitcast_convert_fusion
  143.7 16.3 %convert_reduce_fusion.1 = f32[2048]{0:T(1024)S(1)} fusion(bf16[2048,1,1,64]{3,2,1,0:T(2,128)(2,1)} %reshape.704), kind=kLoop, calls=%fused_computation.186 | loop fusion | flops 260096 | bytes 270336 | tf_op jit(solution)/shard_map/reduce_sum | solution.py:22
  173.0 10.4 %all_to_all.74 = bf16[1,256,8,64]{1,3,0,2:T(8,128)(2,1)S(1)} all-to-all(bf16[1,256,8,64]{1,3,0,2:T(8,128)(2,1)S(1)} %bitcast.251), channel_id=1, replica_groups=mesh['wide'=32,'narrow'=8] {'narrow'}, dimensions={2} | all-to-all | bytes 524288 | tf_op jit(solution)/shard_map/all_to_all | solution.py:147
  185.5 4.4 %select_convert_fusion.3 = bf16[512,2048]{1,0:T(8,128)(2,1)S(1)} fusion(f32[512,2048]{1,0:T(8,128)} %get-tuple-element.20, pred[512]{0:T(512)(128)(4,1)S(1)} %get-tuple-element.23, bf16[1,2048,1,64]{1,3,2,0:T(8,128)(2,1)S(1)} %bitcast.254, bf16[1,2048,1,192]{1,3,2,0:T(8,128)(2,1)S(1)} %bitcast.226), kind=kOutput, calls=%fused_computation.13 | convolution fusion | flops 147849216 | bytes 6619648 | tf_op jit(solution)/shard_map/sbhd,skhd->shbk/dot_general | solution.py:156
  197.9 2.9 select_convert_fusion.1
  201.6 2.9 select_convert_fusion
  206.8 3.7 %copy.81 = bf16[1,2048,1,192]{3,2,0,1:T(2,128)(2,1)} copy(bf16[1,2048,1,192]{1,3,2,0:T(8,128)(2,1)S(1)} %pad_maximum_fusion) | data formatting | bytes 1572864 | tf_op jit(solution)/shard_map/concatenate | solution.py:178
  210.5 12.8 %reduce.13 = bf16[2048,192]{1,0:T(8,128)(2,1)S(1)} reduce(bf16[2048,1,1,192]{3,2,1,0:T(2,128)(2,1)} %bitcast.238, bf16[]{:T(256)} %broadcast.501), dimensions={1,2}, to_apply=%bitcast.171.reduce_sub_computation | reduce | bytes 1572866
  225.4 4.5 %all-to-all-start.5 = ((bf16[8,2,24576]{2,1,0:T(2,128)(2,1)}), bf16[8,2,24576]{2,1,0:T(2,128)(2,1)S(1)}, u32[]{:S(2)}, u32[]{:S(2)}) async-start(bf16[8,2,24576]{2,1,0:T(2,128)(2,1)} %reshape.705), calls=%async_computation.5 | async-start | bytes 1572864 | tf_op jit(solution)/shard_map/all_to_all | solution.py:187
  230.1 12.1 %all-to-all-done.5 = bf16[8,2,24576]{2,1,0:T(2,128)(2,1)S(1)} async-done(((bf16[8,2,24576]{2,1,0:T(2,128)(2,1)}), bf16[8,2,24576]{2,1,0:T(2,128)(2,1)S(1)}, u32[]{:S(2)}, u32[]{:S(2)}) %all-to-all-start.5) | async-done | bytes 786464 | tf_op jit(solution)/shard_map/all_to_all | solution.py:187
  242.2 3.7 reshape.706
  245.9 4.5 %copy.82 = bf16[1,2048,1,192]{1,3,2,0:T(8,128)(2,1)S(1)} copy(bf16[1,2048,1,192]{3,2,0,1:T(2,128)(2,1)} %bitcast.239) | data formatting | bytes 1572864 | tf_op jit(solution)/shard_map/all_to_all | solution.py:187
  252.8 3.1 copy.85
  262.5 19.3 %all_to_all.75 = bf16[32,16,512]{2,1,0:T(8,128)(2,1)S(1)} all-to-all(bf16[32,16,512]{2,1,0:T(8,128)(2,1)S(1)} %bitcast.249), channel_id=1, replica_groups=mesh['wide'=32,'narrow'=8] {'wide'}, dimensions={0} | all-to-all | bytes 1048576 | tf_op jit(solution)/shard_map/all_to_all | solution.py:211
  281.9 5.9 %scatter_custom_fusion.2 = f32[2048,512]{1,0:T(8,128)} fusion(s32[512]{0:T(512)S(1)} %bitcast.265, f32[]{:T(128)} %constant.86.clone.1, bf16[512,512]{1,0:T(8,128)(2,1)S(1)} %bitcast.248), kind=kCustom, calls=%fused_computation.43 | custom fusion | flops 524288 | bytes 4718596 | tf_op jit(solution)/shard_map/scatter-add | solution.py:217
  287.8 3.8 %convert_element_type.227 = bf16[2048,512]{1,0:T(8,128)(2,1)} convert(f32[2048,512]{1,0:T(8,128)} %scatter_custom_fusion.2) | non-fusion elementwise | flops 1048576 | bytes 6291456 | tf_op jit(solution)/shard_map/convert_element_type | solution.py:219
  293.8 63.7 %all-reduce.2.cloned.1.call-done = bf16[2048,512]{1,0:T(8,128)(2,1)} async-done(((bf16[2048,512]{1,0:T(8,128)(2,1)}), bf16[2048,512]{1,0:T(8,128)(2,1)}) %all-reduce.2.cloned.1.call-update) | async-done | bytes 2097168 | tf_op jit(solution)/shard_map/psum | solution.py:219
  360.1 5.5 %fusion.1 = f32[2048,512]{1,0:T(8,128)} fusion(f32[2048,512]{1,0:T(8,128)} %param.7, bf16[2048,512]{1,0:T(8,128)(2,1)} %all-reduce.2.cloned.1.call-done, f32[2048]{0:T(1024)S(1)} %get-tuple-element.7), kind=kLoop, calls=%fused_computation.8 | loop fusion | flops 4194304 | bytes 10493952 | tf_op jit(solution)/shard_map/sub | solution.py:37
  (129 shorter events, 68.8 us)
Async XLA Ops:
  7.2 51.1 %copy-start = (bf16[512,2048]{1,0:T(8,128)(2,1)S(1)}, bf16[512,2048]{1,0:T(8,128)(2,1)}, u32[]{:S(2)}) copy-start(bf16[512,2048]{1,0:T(8,128)(2,1)} %param.11) | copy-start | bytes 6291460
  38.2 18.6 %all-to-all-start.1 = ((bf16[32,16,512]{2,1,0:T(8,128)(2,1)}), bf16[32,16,512]{2,1,0:T(8,128)(2,1)S(1)}, u32[]{:S(2)}, u32[]{:S(2)}) async-start(bf16[32,16,512]{2,1,0:T(8,128)(2,1)} %bitcast.9), calls=%async_computation.1 | async-start | bytes 1048576 | tf_op jit(solution)/shard_map/all_to_all | solution.py:65
  59.0 1.4 copy-start.1
  67.5 21.5 %all-to-all-start.2 = ((bf16[1,256,8,192]{1,3,0,2:T(8,128)(2,1)}), bf16[1,256,8,192]{1,3,0,2:T(8,128)(2,1)S(1)}, u32[]{:S(2)}, u32[]{:S(2)}) async-start(bf16[1,256,8,192]{1,3,0,2:T(8,128)(2,1)} %fusion.36), calls=%async_computation.2 | async-start | bytes 1572864 | tf_op jit(solution)/shard_map/all_to_all | solution.py:80
  88.9 0.9 copy-start.11
  94.6 4.4 %copy-start.2 = (bf16[512,2048]{1,0:T(8,128)(2,1)}, bf16[512,2048]{1,0:T(8,128)(2,1)S(1)}, u32[]{:S(2)}) copy-start(bf16[512,2048]{1,0:T(8,128)(2,1)S(1)} %get-tuple-element.17) | copy-start | bytes 6291460
  98.9 4.4 %copy-start.8 = (bf16[512,2048]{1,0:T(8,128)(2,1)}, bf16[512,2048]{1,0:T(8,128)(2,1)S(1)}, u32[]{:S(2)}) copy-start(bf16[512,2048]{1,0:T(8,128)(2,1)S(1)} %get-tuple-element.19) | copy-start | bytes 6291460
  103.3 4.3 %copy-start.4 = (bf16[512,2048]{1,0:T(8,128)(2,1)}, bf16[512,2048]{1,0:T(8,128)(2,1)S(1)}, u32[]{:S(2)}) copy-start(bf16[512,2048]{1,0:T(8,128)(2,1)S(1)} %get-tuple-element.15) | copy-start | bytes 6291460
  107.6 1.3 copy-start.6
  127.9 11.0 %all-to-all-start.3 = ((bf16[8,2,8192]{2,1,0:T(2,128)(2,1)}), bf16[8,2,8192]{2,1,0:T(2,128)(2,1)S(1)}, u32[]{:S(2)}, u32[]{:S(2)}) async-start(bf16[8,2,8192]{2,1,0:T(2,128)(2,1)} %reshape.703), calls=%async_computation.3 | async-start | bytes 524288 | tf_op jit(solution)/shard_map/all_to_all | solution.py:122
  140.7 27.0 %copy-start.14 = (bf16[1,256,512]{2,1,0:T(8,128)(2,1)S(1)}, bf16[1,256,512]{2,1,0:T(8,128)(2,1)}, u32[]{:S(2)}) copy-start(bf16[1,256,512]{2,1,0:T(8,128)(2,1)} %param.13) | copy-start | bytes 786436
  166.5 4.5 %copy-start.9 = (f32[256,512]{1,0:T(8,128)S(1)}, f32[256,512]{1,0:T(8,128)}, u32[]{:S(2)}) copy-start(f32[256,512]{1,0:T(8,128)} %copy.77) | copy-start | bytes 1572868
  170.3 0.7 copy-start.12
  189.9 1.6 copy-start.3
  189.9 2.2 copy-start.5
  190.4 2.5 copy-start.7
  191.5 2.7 copy-start.17
  194.2 3.7 copy-start.19
  197.9 3.7 copy-start.18
  225.4 16.8 %all-to-all-start.5 = ((bf16[8,2,24576]{2,1,0:T(2,128)(2,1)}), bf16[8,2,24576]{2,1,0:T(2,128)(2,1)S(1)}, u32[]{:S(2)}, u32[]{:S(2)}) async-start(bf16[8,2,24576]{2,1,0:T(2,128)(2,1)} %reshape.705), calls=%async_computation.5 | async-start | bytes 1572864 | tf_op jit(solution)/shard_map/all_to_all | solution.py:187
  229.9 127.6 %all-reduce.2.cloned.1.call-start = ((), (), s32[]{:S(2)}) async-start(), calls=%async_computation.7 | async-start | bytes 4194304 | tf_op jit(solution)/shard_map/psum | solution.py:219
  252.8 5.6 %copy-start.16 = (bf16[256,512]{1,0:T(8,128)(2,1)S(1)}, bf16[256,512]{1,0:T(8,128)(2,1)}, u32[]{:S(2)}) copy-start(bf16[256,512]{1,0:T(8,128)(2,1)} %get-tuple-element.10) | copy-start | bytes 786436
  287.8 3.9 %copy-start.10 = (f32[256,512]{1,0:T(8,128)S(1)}, f32[256,512]{1,0:T(8,128)}, u32[]{:S(2)}) copy-start(f32[256,512]{1,0:T(8,128)} %copy.77) | copy-start | bytes 1572868
  287.8 3.9 %copy-start.13 = (bf16[256,512]{1,0:T(8,128)(2,1)S(1)}, bf16[256,512]{1,0:T(8,128)(2,1)}, u32[]{:S(2)}) copy-start(bf16[256,512]{1,0:T(8,128)(2,1)} %copy-done.12) | copy-start | bytes 786436
  291.6 67.9 %copy-start.15 = (f32[2048]{0:T(1024)S(1)}, f32[2048]{0:T(1024)}, u32[]{:S(2)}) copy-start(f32[2048]{0:T(1024)} %param.8) | copy-start | bytes 24580
Sparse Core Ops, SparseCore 0:
  291.7 65.6 all-reduce.1
where the time goes:
time: 380 us; the launch traced here: 373 us
  waiting for transfers between devices  108 us (28%)
  other arithmetic  77.8 us (20%)
  local copies, waits for them, and re-layouts  53.2 us (14%)
  blocking collectives  50 us (13%)
  matrix products  46 us (12%)
  starting transfers between devices  22 us (6%)
  between operations  15.3 us (4%)
    psum x1, waiting for transfers between devices, local(): lax.psum(row_grads.astype(jnp.bfloat16), 'narrow').astype(jnp.float32)  63.7 us
    unnamed x2, other arithmetic  26.4 us
    all_to_all x1, blocking collectives, local(): lax.all_to_all(requests, 'wide', split_axis=0, concat_axis=0, tiled=True)  20.2 us
    all_to_all x1, blocking collectives, local(): lax.all_to_all(outgoing.astype(jnp.bfloat16), 'wide', split_axis=0, conca...  19.3 us
    unnamed x46, local copies, waits for them, and re-layouts  16.7 us
    reduce_sum x3, other arithmetic, layer_norm(): center = value - jnp.mean(value, axis=-1, keepdims=True)  16.4 us
    all_to_all x1, waiting for transfers between devices, local(): lax.all_to_all(fetched, 'wide', split_axis=0, concat_axis=0, tiled=True)  14.5 us
    dot_general x4, matrix products, block_scores(): jnp.einsum('sbhd,skhd->shbk', queries[:, start:start + block], keys_all,...  14.3 us
  transfers between devices with their start and end apart: 5, of which 5 were waited for; matrix products, arithmetic and copies ran while one was open for 1% of the time, Pallas kernels for 0%

commit v1 on v0

v1 whole, which is shorter than its diff:
```python
import functools

import jax
import jax.numpy as jnp
from jax import lax
from jax.experimental import pallas as pl
from jax.experimental.pallas import tpu as pltpu
from jax.sharding import PartitionSpec as P

HEADS = 8
HD = 64
CAP = 16
EPS = 1e-05
RATE = 0.5
MESH = pl.DeviceIdType.MESH
F32 = jnp.float32
BF16 = jnp.bfloat16
MIB = 1 << 20

NN = (((1,), (0,)), ((), ()))
NT = (((1,), (1,)), ((), ()))
TN = (((0,), (0,)), ((), ()))


def mm(a, b, dims=NN):
    return lax.dot_general(a, b, dims, preferred_element_type=F32)


def iota(shape, dim):
    return lax.broadcasted_iota(jnp.int32, shape, dim)


def sigmoid(t):
    return 0.5 * jnp.tanh(0.5 * t) + 0.5


def silu(t):
    return t * sigmoid(t)


def silu_slope(t):
    s = sigmoid(t)
    return s * (1.0 + t * (1.0 - s))


def greet(axis, me, n):
    barrier = pltpu.get_barrier_semaphore()

    def one(k, carry):
        pl.semaphore_signal(
            barrier, inc=1, device_id={axis: lax.rem(me + k, n)}, device_id_type=MESH
        )
        return carry

    lax.fori_loop(1, n, one, 0)
    return lambda: pl.semaphore_wait(barrier, n - 1)


def remote(src, dst, send_sem, recv_sem, axis, peer):
    return pltpu.make_async_remote_copy(
        src_ref=src,
        dst_ref=dst,
        send_sem=send_sem,
        recv_sem=recv_sem,
        device_id={axis: peer},
        device_id_type=MESH,
    )


def fetch_kernel(
    n, table_ref, ids_ref, emb_ref, target_ref, lanes_ref,
    tab, tabb, asks, asked, picks, reply, replies, tab_sem, ss, rs, ss2, rs2,
):
    me = lax.axis_index("wide")
    greeted = greet("wide", me, n)
    rows_dev = table_ref.shape[0]
    tokens = ids_ref.shape[1]
    load = pltpu.make_async_copy(table_ref, tab, tab_sem)
    load.start()

    ids = ids_ref[...]
    owner = ids // rows_dev
    row = ids - owner * rows_dev
    hits = owner == iota((n, tokens), 0)
    hits_f = hits.astype(F32)
    before = (iota((tokens, tokens), 0) < iota((tokens, tokens), 1)).astype(F32).astype(BF16)
    earlier = mm(hits_f.astype(BF16), before)
    slot = jnp.sum(earlier * hits_f, axis=0, keepdims=True).astype(jnp.int32)
    target = owner * CAP + slot
    target_ref[...] = target
    place = slot + CAP * lax.rem(me, 8)
    at_place = (place == iota((128, tokens), 0)).astype(F32).astype(BF16)
    high = row // 256
    low = row - high * 256
    high_m = (hits_f * high.astype(F32)).astype(BF16)
    low_m = (hits_f * low.astype(F32)).astype(BF16)
    wanted = (mm(high_m, at_place, NT) * 256.0 + mm(low_m, at_place, NT)).astype(jnp.int32)
    for o in range(n):
        asks[o] = wanted[o : o + 1, :]

    greeted()

    def ask(k):
        peer = lax.rem(me + k, n)
        return remote(asks.at[peer], asked.at[me], ss.at[k], rs.at[k], "wide", peer)

    lax.fori_loop(1, n, lambda k, c: (ask(k).start(), c)[1], 0)
    asked[me] = asks[me]
    load.wait()
    tabb[...] = tab[...].astype(BF16)
    lax.fori_loop(1, n, lambda k, c: (ask(k).wait_recv(), c)[1], 0)

    lane16 = iota((CAP, 128), 1)
    sub16 = iota((CAP, 128), 0)
    row_iota = iota((CAP, rows_dev), 1)
    for k in range(n):
        peer = lax.rem(me + k, n)
        line = jnp.broadcast_to(asked[peer], (CAP, 128)).astype(F32)
        mine = lane16 == sub16 + CAP * lax.rem(peer, 8)
        column = jnp.sum(jnp.where(mine, line, 0.0), axis=1, keepdims=True).astype(jnp.int32)
        picks[CAP * k : CAP * (k + 1), :] = (column == row_iota).astype(F32).astype(BF16)
    for g in range(n // 8):
        total = asked[8 * g]
        for j in range(1, 8):
            total = total + asked[8 * g + j]
        lanes_ref[g : g + 1, :] = total
    if n // 8 < 8:
        lanes_ref[n // 8 :, :] = jnp.zeros((8 - n // 8, 128), jnp.int32)

    def answer(k):
        peer = lax.rem(me + k, n)
        return remote(
            reply.at[pl.ds(pl.multiple_of(k * CAP, CAP), CAP)],
            replies.at[pl.ds(pl.multiple_of(me * CAP, CAP), CAP)],
            ss2.at[k],
            rs2.at[k],
            "wide",
            peer,
        )

    half = n // 2
    for part in range(2):
        lo = part * half * CAP
        reply[lo : lo + half * CAP, :] = mm(picks[lo : lo + half * CAP, :], tabb[...]).astype(BF16)
        lax.fori_loop(
            max(1, part * half), (part + 1) * half, lambda k, c: (answer(k).start(), c)[1], 0
        )
    replies[pl.ds(pl.multiple_of(me * CAP, CAP), CAP), :] = reply[:CAP, :]

    target_t = jnp.transpose(jnp.broadcast_to(target.astype(F32), (128, tokens))).astype(jnp.int32)
    take = jnp.concatenate(
        [
            (target_t == iota((tokens, 128), 1) + 128 * g).astype(F32).astype(BF16)
            for g in range(n * CAP // 128)
        ],
        axis=1,
    )
    lax.fori_loop(1, n, lambda k, c: (answer(k).wait_recv(), c)[1], 0)
    emb_ref[...] = mm(take, replies[...]).astype(BF16)

    def done(k, c):
        ask(k).wait_send()
        answer(k).wait_send()
        return c

    lax.fori_loop(1, n, done, 0)


def fetch(n, table, ids):
    rows_dev, width = table.shape
    tokens = ids.shape[1]
    vmem = pl.BlockSpec(memory_space=pltpu.VMEM)
    return pl.pallas_call(
        functools.partial(fetch_kernel, n),
        out_shape=(
            jax.ShapeDtypeStruct((tokens, width), BF16),
            jax.ShapeDtypeStruct((1, tokens), jnp.int32),
            jax.ShapeDtypeStruct((8, 128), jnp.int32),
        ),
        in_specs=[pl.BlockSpec(memory_space=pl.ANY), vmem],
        out_specs=(vmem, vmem, vmem),
        scratch_shapes=[
            pltpu.VMEM((rows_dev, width), F32),
            pltpu.VMEM((rows_dev, width), BF16),
            pltpu.VMEM((n, 1, 128), jnp.int32),
            pltpu.VMEM((n, 1, 128), jnp.int32),
            pltpu.VMEM((n * CAP, rows_dev), BF16),
            pltpu.VMEM((n * CAP, width), BF16),
            pltpu.VMEM((n * CAP, width), BF16),
            pltpu.SemaphoreType.DMA,
            pltpu.SemaphoreType.DMA((n,)),
            pltpu.SemaphoreType.DMA((n,)),
            pltpu.SemaphoreType.DMA((n,)),
            pltpu.SemaphoreType.DMA((n,)),
        ],
        compiler_params=pltpu.CompilerParams(
            collective_id=0, has_side_effects=True, vmem_limit_bytes=32 * MIB
        ),
    )(table, ids)


def norm_back(grad, normed, inverse):
    return inverse * (
        grad
        - jnp.mean(grad, axis=0, keepdims=True)
        - normed * jnp.mean(grad * normed, axis=0, keepdims=True)
    )


def layer_kernel(
    n, emb_ref, len_ref, w_ref, wo_ref, cot_ref, out_ref, ge_ref,
    hid, normed1, qkv_out, qkv, keys, vals, wts, slopes, heads_out, heads, gm, gu,
    gatt_out, gatt, dq, back_out, back, gh, ss, rs,
):
    me = lax.axis_index("narrow")
    greeted = greet("narrow", me, n)
    tokens, width = emb_ref.shape
    att = HEADS * HD
    length = len_ref[0]

    def exchange(step, source, landing, peer):
        return remote(
            source.at[peer], landing.at[me], ss.at[step, peer], rs.at[step, me], "narrow", peer
        )

    def arrived(step, source, landing, peer):
        return pltpu.make_async_remote_copy(
            src_ref=source.at[peer],
            dst_ref=landing.at[peer],
            send_sem=ss.at[step, peer],
            recv_sem=rs.at[step, peer],
            device_id={"narrow": peer},
            device_id_type=MESH,
        )

    def wait_all(step, source, landing):
        def one(k, c):
            arrived(step, source, landing, lax.rem(me + k, n)).wait_recv()
            return c

        lax.fori_loop(1, n, one, 0)

    emb_t = jnp.transpose(emb_ref[...].astype(F32))
    center = emb_t - jnp.mean(emb_t, axis=0, keepdims=True)
    inverse1 = lax.rsqrt(jnp.mean(center * center, axis=0, keepdims=True) + EPS)
    normed = center * inverse1
    normed1[...] = normed
    normed_b = normed.astype(BF16)
    chunk = 256
    total = w_ref.shape[1]
    for c in range(att // chunk, total // chunk):
        hid[c * chunk : (c + 1) * chunk, :] = mm(w_ref[:, c * chunk : (c + 1) * chunk], normed_b, TN)
    greeted()

    def send_head(k, carry):
        peer = lax.rem(me + k, n)
        base = pl.multiple_of(att + 3 * HD * peer, HD)
        qkv_out[peer, :HD, :] = hid[pl.ds(base, HD), :].astype(BF16)
        qkv_out[peer, HD:, :] = silu(hid[pl.ds(base + HD, 2 * HD), :]).astype(BF16)
        exchange(0, qkv_out, qkv, peer).start()
        return carry

    lax.fori_loop(1, n, send_head, 0)
    base = pl.multiple_of(att + 3 * HD * me, HD)
    qkv[me, :HD, :] = hid[pl.ds(base, HD), :].astype(BF16)
    qkv[me, HD:, :] = silu(hid[pl.ds(base + HD, 2 * HD), :]).astype(BF16)

    for c in range(att // chunk):
        hid[c * chunk : (c + 1) * chunk, :] = mm(w_ref[:, c * chunk : (c + 1) * chunk], normed_b, TN)
    live = iota((tokens, 1), 0) + me * tokens < length
    upstream = jnp.where(live, cot_ref[...], jnp.zeros((), BF16))
    gm[...] = mm(wo_ref[...], upstream, NT)
    wait_all(0, qkv_out, qkv)

    scale = HD**-0.5
    for b in range(n):
        vals[b] = jnp.transpose(qkv[b, :HD, :].astype(F32)).astype(BF16)
        keys[b] = jnp.transpose(qkv[b, 2 * HD :, :].astype(F32)).astype(BF16)
    causal = iota((tokens, tokens), 0) <= iota((tokens, tokens), 1)
    for i in range(n):
        query = qkv[i, HD : 2 * HD, :] * scale
        attended = jnp.zeros((HD, tokens), F32)
        for j in range(i + 1):
            scores = mm(keys[j], query)
            s = sigmoid(scores)
            weight = scores * s
            slope = s + weight * (1.0 - s)
            if i == j:
                weight = jnp.where(causal, weight, 0.0)
                slope = jnp.where(causal, slope, 0.0)
            weight = weight.astype(BF16)
            wts[j, i] = weight
            slopes[j, i] = slope.astype(BF16)
            attended = attended + mm(qkv[j, :HD, :], weight)
        heads_out[i] = attended.astype(BF16)

        @pl.when(i != me)
        def _():
            exchange(1, heads_out, heads, i).start()

        @pl.when(i == me)
        def _():
            heads[i] = heads_out[i]

    wait_all(1, heads_out, heads)

    merged = heads[...].astype(F32).reshape(att, tokens)
    center = merged - jnp.mean(merged, axis=0, keepdims=True)
    inverse2 = lax.rsqrt(jnp.mean(center * center, axis=0, keepdims=True) + EPS)
    normed2 = center * inverse2
    gate = silu(hid[:att, :]).astype(BF16).astype(F32)
    grad_mixed = gm[...]
    gu[...] = grad_mixed * normed2
    grad_att = norm_back(grad_mixed * gate, normed2, inverse2).astype(BF16)
    gatt_out[...] = grad_att.reshape(n, HD, tokens)

    def send_grad(k, carry):
        exchange(2, gatt_out, gatt, lax.rem(me + k, n)).start()
        return carry

    lax.fori_loop(1, n, send_grad, 0)
    gatt[me] = gatt_out[me]
    mixed = jnp.transpose(normed2 * gate).astype(BF16)
    result = emb_ref[...].astype(F32) + mm(mixed, wo_ref[...])
    out_ref[...] = jnp.where(live, result, 0.0).astype(BF16)
    wait_all(2, gatt_out, gatt)

    dq[...] = jnp.zeros_like(dq)
    for j in range(n):
        dv = jnp.zeros((HD, tokens), F32)
        dk = jnp.zeros((HD, tokens), F32)
        for i in range(j, n):
            grad = gatt[i]
            dw = mm(vals[j], grad)
            ds = (dw * slopes[j, i].astype(F32)).astype(BF16)
            dv = dv + mm(grad, wts[j, i], NT)
            dk = dk + mm(qkv[i, HD : 2 * HD, :], ds, NT)
            dq[i] += mm(qkv[j, 2 * HD :, :], ds)
        back_out[j, :HD, :] = dv.astype(BF16)
        back_out[j, HD : 2 * HD, :] = (dq[j] * scale).astype(BF16)
        back_out[j, 2 * HD :, :] = (dk * scale).astype(BF16)

        @pl.when(j != me)
        def _():
            exchange(3, back_out, back, j).start()

        @pl.when(j == me)
        def _():
            back[j] = back_out[j]

    gh[:att, :] = (gu[...] * silu_slope(hid[:att, :])).astype(BF16)
    upstream_t = jnp.transpose(upstream.astype(F32))
    wait_all(3, back_out, back)
    for h in range(HEADS):
        base = att + 3 * HD * h
        gh[base : base + HD, :] = back[h, :HD, :]
        gh[base + HD : base + 3 * HD, :] = (
            back[h, HD:, :].astype(F32) * silu_slope(hid[base + HD : base + 3 * HD, :])
        ).astype(BF16)
    grad_norm1 = mm(w_ref[...], gh[...])
    grad_emb = norm_back(grad_norm1, normed1[...], inverse1) + upstream_t
    live_t = iota((1, tokens), 1) + me * tokens < length
    ge_ref[...] = jnp.where(live_t, grad_emb, 0.0).astype(BF16)

    def done(k, c):
        peer = lax.rem(me + k, n)
        arrived(0, qkv_out, qkv, peer).wait_send()
        arrived(1, heads_out, heads, peer).wait_send()
        arrived(2, gatt_out, gatt, peer).wait_send()
        arrived(3, back_out, back, peer).wait_send()
        return c

    lax.fori_loop(1, n, done, 0)


def layer(n, emb, lengths, w_uvqk, w_out, cotangent):
    tokens, width = emb.shape
    att = HEADS * HD
    vmem = pl.BlockSpec(memory_space=pltpu.VMEM)
    return pl.pallas_call(
        functools.partial(layer_kernel, n),
        out_shape=(
            jax.ShapeDtypeStruct((tokens, width), BF16),
            jax.ShapeDtypeStruct((width, tokens), BF16),
        ),
        in_specs=[vmem, pl.BlockSpec(memory_space=pltpu.SMEM), vmem, vmem, vmem],
        out_specs=(vmem, vmem),
        scratch_shapes=[
            pltpu.VMEM((4 * att, tokens), F32),
            pltpu.VMEM((width, tokens), F32),
            pltpu.VMEM((n, 3 * HD, tokens), BF16),
            pltpu.VMEM((n, 3 * HD, tokens), BF16),
            pltpu.VMEM((n, tokens, HD), BF16),
            pltpu.VMEM((n, tokens, HD), BF16),
            pltpu.VMEM((n, n, tokens, tokens), BF16),
            pltpu.VMEM((n, n, tokens, tokens), BF16),
            pltpu.VMEM((n, HD, tokens), BF16),
            pltpu.VMEM((n, HD, tokens), BF16),
            pltpu.VMEM((att, tokens), F32),
            pltpu.VMEM((att, tokens), F32),
            pltpu.VMEM((n, HD, tokens), BF16),
            pltpu.VMEM((n, HD, tokens), BF16),
            pltpu.VMEM((n, HD, tokens), F32),
            pltpu.VMEM((n, 3 * HD, tokens), BF16),
            pltpu.VMEM((n, 3 * HD, tokens), BF16),
            pltpu.VMEM((4 * att, tokens), BF16),
            pltpu.SemaphoreType.DMA((4, n)),
            pltpu.SemaphoreType.DMA((4, n)),
        ],
        compiler_params=pltpu.CompilerParams(
            collective_id=1, has_side_effects=True, vmem_limit_bytes=48 * MIB
        ),
    )(emb, lengths, w_uvqk, w_out, cotangent)


def scatter_kernel(
    n, ge_ref, target_ref, lanes_ref, part_ref, outgoing, arriving, hot, ss, rs
):
    me = lax.axis_index("wide")
    greeted = greet("wide", me, n)
    rows_dev = part_ref.shape[0]
    tokens = ge_ref.shape[1]
    slots = n * CAP
    put = (iota((slots, tokens), 0) == target_ref[...]).astype(F32).astype(BF16)
    outgoing[...] = mm(put, ge_ref[...], NT).astype(BF16)
    greeted()

    def give(k):
        peer = lax.rem(me + k, n)
        return remote(
            outgoing.at[pl.ds(pl.multiple_of(peer * CAP, CAP), CAP)],
            arriving.at[pl.ds(pl.multiple_of(me * CAP, CAP), CAP)],
            ss.at[k],
            rs.at[k],
            "wide",
            peer,
        )

    lax.fori_loop(1, n, lambda k, c: (give(k).start(), c)[1], 0)
    own = pl.ds(pl.multiple_of(me * CAP, CAP), CAP)
    arriving[own, :] = outgoing[own, :]
    for g in range(slots // 128):
        hot[:, 128 * g : 128 * (g + 1)] = (
            (iota((rows_dev, 128), 0) == lanes_ref[g : g + 1, :]).astype(F32).astype(BF16)
        )
    lax.fori_loop(1, n, lambda k, c: (give(k).wait_recv(), c)[1], 0)
    part_ref[...] = mm(hot[...], arriving[...]).astype(BF16)
    lax.fori_loop(1, n, lambda k, c: (give(k).wait_send(), c)[1], 0)


def scatter(n, rows_dev, grad_emb, target, lanes):
    width, tokens = grad_emb.shape
    vmem = pl.BlockSpec(memory_space=pltpu.VMEM)
    return pl.pallas_call(
        functools.partial(scatter_kernel, n),
        out_shape=jax.ShapeDtypeStruct((rows_dev, width), BF16),
        in_specs=[vmem, vmem, vmem],
        out_specs=vmem,
        scratch_shapes=[
            pltpu.VMEM((n * CAP, width), BF16),
            pltpu.VMEM((n * CAP, width), BF16),
            pltpu.VMEM((rows_dev, n * CAP), BF16),
            pltpu.SemaphoreType.DMA((n,)),
            pltpu.SemaphoreType.DMA((n,)),
        ],
        compiler_params=pltpu.CompilerParams(
            collective_id=2, has_side_effects=True, vmem_limit_bytes=32 * MIB
        ),
    )(grad_emb, target, lanes)


def sum_kernel(n, part_ref, sum_ref, sib_in, half_sum, blocks_in, ss, rs):
    me = lax.axis_index("narrow")
    greeted = greet("narrow", me, n)
    chip = me // 2
    core = lax.rem(me, 2)
    sibling = chip * 2 + 1 - core
    chips = n // 2
    rows_dev, width = part_ref.shape
    half = rows_dev // 2
    block = half // chips
    greeted()

    def rows(ref, start, size):
        return ref.at[pl.ds(pl.multiple_of(start, block), size)]

    swap = remote(
        rows(part_ref, (1 - core) * half, half), sib_in, ss.at[0], rs.at[0], "narrow", sibling
    )
    swap.start()
    swap.wait_recv()
    half_sum[...] = (
        part_ref[pl.ds(pl.multiple_of(core * half, block), half), :].astype(F32)
        + sib_in[...].astype(F32)
    ).astype(BF16)

    def spread(k):
        other = lax.rem(chip + k, chips)
        return remote(
            rows(half_sum, other * block, block),
            blocks_in.at[k],
            ss.at[k],
            rs.at[k],
            "narrow",
            other * 2 + core,
        )

    for k in range(1, chips):
        spread(k).start()
    total = half_sum[pl.ds(pl.multiple_of(chip * block, block), block), :].astype(F32)
    for k in range(1, chips):
        spread(k).wait_recv()
        total = total + blocks_in[k].astype(F32)
    mine = core * half + chip * block
    sum_ref[pl.ds(pl.multiple_of(mine, block), block), :] = total.astype(BF16)

    def collect(k):
        other = lax.rem(chip + k, chips)
        return remote(
            rows(sum_ref, mine, block),
            rows(sum_ref, mine, block),
            ss.at[chips + k],
            rs.at[chips + k],
            "narrow",
            other * 2 + core,
        )

    def pass_on(k):
        source = lax.rem(chip + chips - k, chips)
        start = core * half + source * block
        return remote(
            rows(sum_ref, start, block),
            rows(sum_ref, start, block),
            ss.at[2 * chips + k],
            rs.at[2 * chips + k],
            "narrow",
            sibling,
        )

    for k in range(1, chips):
        collect(k).start()
    pass_on(0).start()
    for k in range(1, chips):
        collect(k).wait_recv()
        pass_on(k).start()
    for k in range(chips):
        pass_on(k).wait_recv()
    swap.wait_send()
    for k in range(1, chips):
        spread(k).wait_send()
        collect(k).wait_send()
    for k in range(chips):
        pass_on(k).wait_send()


def sum_rows(n, partial):
    rows_dev, width = partial.shape
    vmem = pl.BlockSpec(memory_space=pltpu.VMEM)
    half = rows_dev // 2
    chips = n // 2
    return pl.pallas_call(
        functools.partial(sum_kernel, n),
        out_shape=jax.ShapeDtypeStruct((rows_dev, width), BF16),
        in_specs=[vmem],
        out_specs=vmem,
        scratch_shapes=[
            pltpu.VMEM((half, width), BF16),
            pltpu.VMEM((half, width), BF16),
            pltpu.VMEM((chips, half // chips, width), BF16),
            pltpu.SemaphoreType.DMA((3 * chips,)),
            pltpu.SemaphoreType.DMA((3 * chips,)),
        ],
        compiler_params=pltpu.CompilerParams(
            collective_id=3, has_side_effects=True, vmem_limit_bytes=32 * MIB
        ),
    )(partial)


def local(table, accum, ids, lengths, w_uvqk, w_out, cotangent):
    n_wide = lax.axis_size("wide")
    n_narrow = lax.axis_size("narrow")
    rows_dev, width = table.shape
    tokens = ids.shape[1]
    emb, target, lanes = fetch(n_wide, table, ids)
    output, grad_emb = layer(
        n_narrow, emb, lengths, w_uvqk, w_out, cotangent.reshape(tokens, width)
    )
    partial = scatter(n_wide, rows_dev, grad_emb, target, lanes)
    summed = sum_rows(n_narrow, partial).astype(F32)
    new_accum = accum + jnp.mean(summed * summed, axis=1)
    new_table = table - RATE * summed / jnp.sqrt(new_accum)[:, None]
    return (output.reshape(1, tokens, width), new_table, new_accum)


def solution(mesh):
    in_specs = (
        P("wide", None),
        P("wide"),
        P("wide", "narrow"),
        P("wide"),
        P(),
        P(),
        P("wide", "narrow", None),
    )
    out_specs = (P("wide", "narrow", None), P("wide", None), P("wide"))
    return jax.shard_map(local, mesh=mesh, in_specs=in_specs, out_specs=out_specs, check_vma=False)
```

time: 380 us -> 143 us (0.38); the launches traced: 373 us -> 143 us
  Pallas kernels: 0 us -> 134 us
  waiting for transfers between devices: 108 us -> 0 us
  other arithmetic: 77.8 us -> 3.72 us
  blocking collectives: 50 us -> 0 us
  local copies, waits for them, and re-layouts: 53.2 us -> 3.59 us
  matrix products: 46 us -> 0 us
  starting transfers between devices: 22 us -> 0 us
  between operations: 15.3 us -> 1.37 us
    pallas_call x0 -> x4, Pallas kernels: none -> 134 us  [the longest x1 48.9 us: layer(): pl.pallas_call(functools.partial(layer_kernel, n), out_shape=(jax.ShapeDt...]
    psum x1 -> x0, waiting for transfers between devices: 63.7 us -> none  [local(): lax.psum(row_grads.astype(jnp.bfloat16), 'narrow').astype(jnp.float32)]
    all_to_all x3 -> x0, blocking collectives: 50 us -> none  [the longest x1 20.2 us: local(): lax.all_to_all(requests, 'wide', split_axis=0, concat_axis=0, tiled=True)]
    dot_general x28 -> x0, matrix products: 46 us -> none  [the longest x4 14.3 us: block_scores(): jnp.einsum('sbhd,skhd->shbk', queries[:, start:start + block], keys_all,...]
    all_to_all x4 -> x0, waiting for transfers between devices: 44.6 us -> none  [the longest x1 14.5 us: local(): lax.all_to_all(fetched, 'wide', split_axis=0, concat_axis=0, tiled=True)]
    unnamed x2 -> x0, other arithmetic: 26.4 us -> none
    all_to_all x4 -> x0, starting transfers between devices: 22 us -> none  [the longest x1 9.2 us: local(): lax.all_to_all(act_rest.reshape(seq_count, stretch, HEADS, 3 * HD), 'narr...]
    reduce_sum x7 -> x1, other arithmetic: 20 us -> 0.48 us  [local(): new_accum = accum + jnp.mean(summed * summed, axis=1)]
  transfers between devices with their start and end apart: 5 -> 0, of which waited for: 5 -> 0; matrix products, arithmetic and copies ran while one was open for 1% -> 0% of each run, Pallas kernels for 0% -> 0%
where the time goes in v1:
time: 143 us
  Pallas kernels  134 us (94%)
  other arithmetic  3.72 us (3%)
  local copies, waits for them, and re-layouts  3.59 us (3%)
    pallas_call x1, Pallas kernels, layer(): pl.pallas_call(functools.partial(layer_kernel, n), out_shape=(jax.ShapeDt...  48.9 us
    pallas_call x1, Pallas kernels, sum_rows(): pl.pallas_call(functools.partial(sum_kernel, n), out_shape=jax.ShapeDtype...  38.9 us
    pallas_call x1, Pallas kernels, fetch(): pl.pallas_call(functools.partial(fetch_kernel, n), out_shape=(jax.ShapeDt...  28.2 us
    pallas_call x1, Pallas kernels, scatter(): pl.pallas_call(functools.partial(scatter_kernel, n), out_shape=jax.ShapeD...  18.4 us
    unnamed x15, local copies, waits for them, and re-layouts  3.59 us

profile of v1, /device:TPU:1, one launch (start us, length us, event | category | flops | bytes accessed | tf_op | source)
XLA Modules:
  0.0 143.1 jit_solution(16709664899327835984)
XLA Ops:
  1.3 0.0 copy-start
  1.3 2.2 %copy-done = f32[2048,512]{1,0:T(8,128)S(1)} copy-done((f32[2048,512]{1,0:T(8,128)S(1)}, f32[2048,512]{1,0:T(8,128)}, u32[]{:S(2)}) %copy-start) | copy-done | bytes 4194328
  3.5 0.0 copy-start.5
  3.5 0.7 copy-done.5
  4.1 0.0 copy-start.2
  4.2 0.0 copy-start.3
  4.2 0.0 copy-start.4
  4.2 28.2 %shard_map.94 = (bf16[256,512]{1,0:T(8,128)(2,1)S(1)}, s32[1,256]{1,0:T(1,128)S(1)}, s32[8,128]{1,0:T(8,128)S(1)}) custom-call(f32[2048,512]{1,0:T(8,128)S(1)} %copy-done, s32[1,256]{1,0:T(1,128)S(1)} %copy-done.5), custom_call_target="tpu_custom_call" | custom-call | tf_op jit(solution)/shard_map/pallas_call | solution.py:173
  32.4 0.0 copy-done.2
  32.4 0.0 copy-done.3
  32.4 0.0 copy-done.4
  32.4 48.9 %shard_map.95 = (bf16[256,512]{1,0:T(8,128)(2,1)S(1)}, bf16[512,256]{1,0:T(8,128)(2,1)S(1)}) custom-call(bf16[256,512]{1,0:T(8,128)(2,1)S(1)} %get-tuple-element.8.emb_ref, s32[1]{0:T(128)S(6)} %copy.11.len_ref, bf16[512,2048]{1,0:T(8,128)(2,1)S(1)} %copy-done.2, bf16[512,512]{1,0:T(8,128)(2,1)S(1)} %copy-done.3, bf16[256,512]{1,0:T(8,128)(2,1)S(1)} %bitcast.3), custom_call_target="tpu_custom_call" | custom-call | tf_op jit(solution)/shard_map/pallas_call | solution.py:380
  81.4 0.0 copy-start.6
  81.4 0.0 copy-start.1
  81.4 18.4 %shard_map.96.part_ref = bf16[2048,512]{1,0:T(8,128)(2,1)S(1)} custom-call(bf16[512,256]{1,0:T(8,128)(2,1)S(1)} %get-tuple-element.10.ge_ref, s32[1,256]{1,0:T(1,128)S(1)} %get-tuple-element.11.target_ref, s32[8,128]{1,0:T(8,128)S(1)} %get-tuple-element.12.lanes_ref), custom_call_target="tpu_custom_call" | custom-call | tf_op jit(solution)/shard_map/pallas_call | solution.py:454
  99.8 38.9 %shard_map.97 = bf16[2048,512]{1,0:T(8,128)(2,1)S(1)} custom-call(bf16[2048,512]{1,0:T(8,128)(2,1)S(1)} %shard_map.96.part_ref), custom_call_target="tpu_custom_call" | custom-call | tf_op jit(solution)/shard_map/pallas_call | solution.py:561
  138.7 0.5 fusion.2
  139.2 0.0 copy-done.6
  139.2 0.6 fusion.3
  139.8 0.0 copy-done.1
  139.8 2.6 %fusion.1 = f32[2048,512]{1,0:T(8,128)} fusion(f32[2048,512]{1,0:T(8,128)S(1)} %copy-done.1, bf16[2048,512]{1,0:T(8,128)(2,1)S(1)} %shard_map.97, f32[2048]{0:T(1024)S(1)} %get-tuple-element.13), kind=kLoop, calls=%fused_computation.3 | loop fusion | flops 4194304 | bytes 10493952 | tf_op jit(solution)/shard_map/sub | solution.py:591
  142.4 0.7 copy.12
Async XLA Ops:
  1.3 2.2 %copy-start = (f32[2048,512]{1,0:T(8,128)S(1)}, f32[2048,512]{1,0:T(8,128)}, u32[]{:S(2)}) copy-start(f32[2048,512]{1,0:T(8,128)} %table_ref.1) | copy-start | bytes 12582916
  3.5 0.7 copy-start.5
  4.1 28.2 %copy-start.2 = (bf16[512,2048]{1,0:T(8,128)(2,1)S(1)}, bf16[512,2048]{1,0:T(8,128)(2,1)}, u32[]{:S(2)}) copy-start(bf16[512,2048]{1,0:T(8,128)(2,1)} %w_ref.1) | copy-start | bytes 6291460
  4.2 28.2 %copy-start.3 = (bf16[512,512]{1,0:T(8,128)(2,1)S(1)}, bf16[512,512]{1,0:T(8,128)(2,1)}, u32[]{:S(2)}) copy-start(bf16[512,512]{1,0:T(8,128)(2,1)} %wo_ref.1) | copy-start | bytes 1572868
  4.2 28.2 %copy-start.4 = (bf16[1,256,512]{2,1,0:T(8,128)(2,1)S(1)}, bf16[1,256,512]{2,1,0:T(8,128)(2,1)}, u32[]{:S(2)}) copy-start(bf16[1,256,512]{2,1,0:T(8,128)(2,1)} %param.13) | copy-start | bytes 786436
  81.4 57.8 %copy-start.6 = (f32[2048]{0:T(1024)S(1)}, f32[2048]{0:T(1024)}, u32[]{:S(2)}) copy-start(f32[2048]{0:T(1024)} %param.8) | copy-start | bytes 24580
  81.4 58.4 %copy-start.1 = (f32[2048,512]{1,0:T(8,128)S(1)}, f32[2048,512]{1,0:T(8,128)}, u32[]{:S(2)}) copy-start(f32[2048,512]{1,0:T(8,128)} %table_ref.1) | copy-start | bytes 12582916

commit v2 on v0

v2 whole, which is shorter than its diff:
```python
import functools

import jax
import jax.numpy as jnp
from jax import lax
from jax.experimental import pallas as pl
from jax.experimental.pallas import tpu as pltpu
from jax.sharding import PartitionSpec as P

HEADS = 8
HD = 64
CAP = 16
EPS = 1e-05
RATE = 0.5
MESH = pl.DeviceIdType.MESH
F32 = jnp.float32
BF16 = jnp.bfloat16
MIB = 1 << 20

NN = (((1,), (0,)), ((), ()))
NT = (((1,), (1,)), ((), ()))
TN = (((0,), (0,)), ((), ()))


def mm(a, b, dims=NN):
    return lax.dot_general(a, b, dims, preferred_element_type=F32)


def iota(shape, dim):
    return lax.broadcasted_iota(jnp.int32, shape, dim)


def sigmoid(t):
    return 0.5 * jnp.tanh(0.5 * t) + 0.5


def silu(t):
    return t * sigmoid(t)


def silu_slope(t):
    s = sigmoid(t)
    return s * (1.0 + t * (1.0 - s))


def norm_back(grad, normed, inverse):
    return inverse * (
        grad
        - jnp.mean(grad, axis=0, keepdims=True)
        - normed * jnp.mean(grad * normed, axis=0, keepdims=True)
    )


def onehot(match):
    return match.astype(F32).astype(BF16)


def each(lower, upper, act):
    def step(k, carry):
        act(k)
        return carry

    lax.fori_loop(lower, upper, step, 0)


def remote(src, dst, send_sem, recv_sem, peer):
    return pltpu.make_async_remote_copy(
        src_ref=src,
        dst_ref=dst,
        send_sem=send_sem,
        recv_sem=recv_sem,
        device_id=peer,
        device_id_type=MESH,
    )


def wait_bytes(ref, sem):
    pltpu.make_async_copy(ref, ref, sem).wait()


def tile16(start):
    return pl.ds(pl.multiple_of(start, CAP), CAP)


def step_kernel(
    n_wide, n, table_ref, ids_ref, len_ref, w_hbm, wo_hbm, cot_hbm, out_ref, sum_ref,
    tab, tabb, w_ref, wo_ref, cot_ref, wt, asks, asked, picks, reply, replies, lanes, hot,
    emb, hid, normed1, qkv_out, qkv, keys, vals, wts, slopes, heads_out, heads, gm, gu,
    gatt_out, gatt, dq, dk, dv, back_out, back, gh, up_t, ge, outgoing, arriving, sib_out, sib_in,
    load_sem, ask_sem, reply_sem, lane_sem, nss, nrs, give_sem, sib_ss, sib_rs, col_ss, col_rs,
    pass_ss, pass_rs,
):
    wide = lax.axis_index("wide")
    me = lax.axis_index("narrow")
    chip = me // 2
    core = lax.rem(me, 2)
    chips = n // 2
    rows_dev, width = table_ref.shape
    tokens = ids_ref.shape[1]
    att = HEADS * HD
    slots = n_wide * CAP
    cols = width // chips

    def at_wide(k):
        return lax.rem(wide + k, n_wide)

    def at_chip(k):
        return lax.rem(chip + k, chips)

    barrier = pltpu.get_barrier_semaphore()

    def hail(peer):
        pl.semaphore_signal(barrier, inc=1, device_id=peer, device_id_type=MESH)

    each(
        1,
        n_wide * chips,
        lambda k: hail({"wide": at_wide(k // chips), "narrow": at_chip(lax.rem(k, chips)) * 2 + core}),
    )
    each(0, chips, lambda k: hail({"wide": wide, "narrow": at_chip(k) * 2 + 1 - core}))

    loads = [
        pltpu.make_async_copy(src, dst, load_sem.at[i])
        for i, (src, dst) in enumerate(
            ((table_ref, tab), (w_hbm, w_ref), (wo_hbm, wo_ref), (cot_hbm, cot_ref))
        )
    ]
    for load in loads:
        load.start()

    ids = ids_ref[...]
    owner = ids // rows_dev
    row = ids - owner * rows_dev
    hits_f = (owner == iota((n_wide, tokens), 0)).astype(F32)
    before = onehot(iota((tokens, tokens), 0) < iota((tokens, tokens), 1))
    earlier = mm(hits_f.astype(BF16), before)
    slot = jnp.sum(earlier * hits_f, axis=0, keepdims=True).astype(jnp.int32)
    target = owner * CAP + slot
    place = slot + CAP * lax.rem(wide, 8)
    at_place = onehot(place == iota((128, tokens), 0))
    high = row // 256
    low = row - high * 256
    high_m = (hits_f * high.astype(F32)).astype(BF16)
    low_m = (hits_f * low.astype(F32)).astype(BF16)
    wanted = (mm(high_m, at_place, NT) * 256.0 + mm(low_m, at_place, NT)).astype(jnp.int32)
    for o in range(n_wide):
        asks[o] = wanted[o : o + 1, :]

    pl.semaphore_wait(barrier, n_wide * chips - 1 + chips)

    def ask(k):
        peer = at_wide(k)
        remote(
            asks.at[peer], asked.at[wide], ask_sem.at[0], ask_sem.at[1], {"wide": peer}
        ).start()

    each(1, n_wide, ask)
    asked[wide] = asks[wide]
    loads[0].wait()
    tabb[...] = tab[...].astype(BF16)
    wait_bytes(asked.at[pl.ds(0, n_wide - 1)], ask_sem.at[1])

    lane16 = iota((CAP, 128), 1)
    sub16 = iota((CAP, 128), 0)
    row_iota = iota((CAP, rows_dev), 1)

    def answer(k):
        peer = at_wide(k)
        remote(
            reply.at[tile16(k * CAP)],
            replies.at[tile16(wide * CAP)],
            reply_sem.at[0],
            reply_sem.at[1],
            {"wide": peer},
        ).start()

    half = n_wide // 2
    for part in range(2):
        for k in range(part * half, (part + 1) * half):
            peer = at_wide(k)
            line = jnp.broadcast_to(asked[peer], (CAP, 128)).astype(F32)
            mine = lane16 == sub16 + CAP * lax.rem(peer, 8)
            column = jnp.sum(jnp.where(mine, line, 0.0), axis=1, keepdims=True).astype(jnp.int32)
            picks[CAP * k : CAP * (k + 1), :] = onehot(column == row_iota)
        lo = part * half * CAP
        reply[lo : lo + half * CAP, :] = mm(picks[lo : lo + half * CAP, :], tabb[...]).astype(BF16)
        each(max(1, part * half), (part + 1) * half, answer)
    replies[tile16(wide * CAP), :] = reply[:CAP, :]

    for g in range(n_wide // 8):
        total = asked[8 * g]
        for j in range(1, 8):
            total = total + asked[8 * g + j]
        lanes[chip, g : g + 1, :] = total
    for k in range(1, chips):
        remote(
            lanes.at[chip], lanes.at[chip], lane_sem.at[0], lane_sem.at[1],
            {"narrow": at_chip(k) * 2 + core},
        ).start()

    target_t = jnp.transpose(jnp.broadcast_to(target.astype(F32), (128, tokens))).astype(jnp.int32)
    take = jnp.concatenate(
        [onehot(target_t == iota((tokens, 128), 1) + 128 * g) for g in range(slots // 128)],
        axis=1,
    )

    length = len_ref[0]
    live = iota((tokens, 1), 0) + me * tokens < length
    live_t = iota((1, tokens), 1) + me * tokens < length
    for load in loads[1:]:
        load.wait()
    chunk = 256
    eye = onehot(iota((chunk, chunk), 0) == iota((chunk, chunk), 1))
    total_w = w_ref.shape[1]
    for c in range(total_w // chunk):
        part = slice(c * chunk, (c + 1) * chunk)
        wt[part, :] = mm(eye, w_ref[:, part], NT).astype(BF16)
    upstream = jnp.where(live, cot_ref[...], jnp.zeros((), BF16))
    gm[...] = mm(wo_ref[...], upstream, NT)
    up_t[...] = jnp.transpose(upstream.astype(F32))
    wait_bytes(lanes.at[pl.ds(0, chips - 1)], lane_sem.at[1])
    for y in range(chips):
        for g in range(slots // 128):
            lo = y * slots + 128 * g
            hot[:, lo : lo + 128] = onehot(iota((rows_dev, 128), 0) == lanes[y, g : g + 1, :])
    wait_bytes(replies.at[pl.ds(0, slots - CAP)], reply_sem.at[1])
    emb[...] = mm(take, replies[...])

    def exchange(step, source, landing, peer):
        return remote(
            source.at[peer],
            landing.at[me],
            nss.at[step, peer],
            nrs.at[step, me],
            {"narrow": peer},
        )

    def arrive(step, landing, peer):
        wait_bytes(landing.at[peer], nrs.at[step, peer])

    emb_t = jnp.transpose(emb[...])
    center = emb_t - jnp.mean(emb_t, axis=0, keepdims=True)
    inverse1 = lax.rsqrt(jnp.mean(center * center, axis=0, keepdims=True) + EPS)
    normed = center * inverse1
    normed1[...] = normed
    normed_b = normed.astype(BF16)
    for c in range(att // chunk, total_w // chunk):
        hid[c * chunk : (c + 1) * chunk, :] = mm(wt[c * chunk : (c + 1) * chunk, :], normed_b)

    def send_head(k):
        peer = lax.rem(me + k, n)
        base = pl.multiple_of(att + 3 * HD * peer, HD)
        qkv_out[peer, :HD, :] = hid[pl.ds(base, HD), :].astype(BF16)
        qkv_out[peer, HD:, :] = silu(hid[pl.ds(base + HD, 2 * HD), :]).astype(BF16)
        exchange(0, qkv_out, qkv, peer).start()

    each(1, n, send_head)
    base = pl.multiple_of(att + 3 * HD * me, HD)
    qkv[me, :HD, :] = hid[pl.ds(base, HD), :].astype(BF16)
    qkv[me, HD:, :] = silu(hid[pl.ds(base + HD, 2 * HD), :]).astype(BF16)

    for c in range(att // chunk):
        hid[c * chunk : (c + 1) * chunk, :] = mm(wt[c * chunk : (c + 1) * chunk, :], normed_b)
    each(1, n, lambda k: arrive(0, qkv, lax.rem(me + k, n)))

    scale = HD**-0.5
    for b in range(n):
        vals[b] = jnp.transpose(qkv[b, :HD, :].astype(F32)).astype(BF16)
        keys[b] = jnp.transpose(qkv[b, 2 * HD :, :].astype(F32)).astype(BF16)
    causal = iota((tokens, tokens), 0) <= iota((tokens, tokens), 1)
    for i in reversed(range(n)):
        query = qkv[i, HD : 2 * HD, :] * scale
        attended = jnp.zeros((HD, tokens), F32)
        for j in range(i + 1):
            scores = mm(keys[j], query)
            s = sigmoid(scores)
            weight = scores * s
            slope = s + weight * (1.0 - s)
            if i == j:
                weight = jnp.where(causal, weight, 0.0)
                slope = jnp.where(causal, slope, 0.0)
            weight = weight.astype(BF16)
            wts[j, i] = weight
            slopes[j, i] = slope.astype(BF16)
            attended = attended + mm(qkv[j, :HD, :], weight)
        heads_out[i] = attended.astype(BF16)

        @pl.when(i != me)
        def _():
            exchange(1, heads_out, heads, i).start()

        @pl.when(i == me)
        def _():
            heads[i] = heads_out[i]

    each(1, n, lambda k: arrive(1, heads, lax.rem(me + k, n)))

    merged = heads[...].astype(F32).reshape(att, tokens)
    center = merged - jnp.mean(merged, axis=0, keepdims=True)
    inverse2 = lax.rsqrt(jnp.mean(center * center, axis=0, keepdims=True) + EPS)
    normed2 = center * inverse2
    gate = silu(hid[:att, :]).astype(BF16).astype(F32)
    grad_mixed = gm[...]
    gu[...] = grad_mixed * normed2
    grad_att = norm_back(grad_mixed * gate, normed2, inverse2).astype(BF16)
    gatt_out[...] = grad_att.reshape(n, HD, tokens)
    each(1, n, lambda k: exchange(2, gatt_out, gatt, lax.rem(me + k, n)).start())
    gatt[me] = gatt_out[me]
    mixed = jnp.transpose(normed2 * gate).astype(BF16)
    result = emb[...] + mm(mixed, wo_ref[...])
    out_ref[...] = jnp.where(live, result, 0.0).astype(BF16)
    gh[:att, :] = (gu[...] * silu_slope(hid[:att, :])).astype(BF16)
    dk[...] = jnp.zeros_like(dk)
    dv[...] = jnp.zeros_like(dv)

    for i in reversed(range(n)):

        @pl.when(i != me)
        def _():
            arrive(2, gatt, i)

        grad = gatt[i]
        query = qkv[i, HD : 2 * HD, :]
        dq = jnp.zeros((HD, tokens), F32)
        for j in range(i + 1):
            dw = mm(vals[j], grad)
            ds = (dw * slopes[j, i].astype(F32)).astype(BF16)
            dv[j] += mm(grad, wts[j, i], NT)
            dk[j] += mm(query, ds, NT)
            dq = dq + mm(qkv[j, 2 * HD :, :], ds)
        back_out[i, :HD, :] = dv[i].astype(BF16)
        back_out[i, HD : 2 * HD, :] = (dq * scale).astype(BF16)
        back_out[i, 2 * HD :, :] = (dk[i] * scale).astype(BF16)

        @pl.when(i != me)
        def _():
            exchange(3, back_out, back, i).start()

        @pl.when(i == me)
        def _():
            back[i] = back_out[i]

    hid[att:, :] = silu_slope(hid[att:, :])
    put = onehot(iota((slots, tokens), 0) == target)
    each(1, n, lambda k: arrive(3, back, lax.rem(me + k, n)))
    for h in range(HEADS):
        base = att + 3 * HD * h
        gh[base : base + HD, :] = back[h, :HD, :]
        gh[base + HD : base + 3 * HD, :] = (
            back[h, HD:, :].astype(F32) * hid[base + HD : base + 3 * HD, :]
        ).astype(BF16)
    grad_norm1 = mm(w_ref[...], gh[...])
    grad_emb = norm_back(grad_norm1, normed1[...], inverse1) + up_t[...]
    ge[...] = jnp.where(live_t, grad_emb, 0.0).astype(BF16)

    own = tile16(chip * slots + wide * CAP)

    def give(k, y):
        o = at_wide(k)
        remote(
            outgoing.at[tile16(y * slots + o * CAP)],
            arriving.at[own],
            give_sem.at[0],
            give_sem.at[1],
            {"wide": o, "narrow": y * 2 + core},
        ).start()

    for q in range(chips):
        y = at_chip(q)
        block = ge[pl.ds(pl.multiple_of(y * cols, cols), cols), :]
        outgoing[pl.ds(pl.multiple_of(y * slots, slots), slots), :] = mm(put, block, NT).astype(BF16)
        each(1 if q == 0 else 0, n_wide, lambda k: give(k, y))
    arriving[own, :] = outgoing[own, :]
    wait_bytes(arriving.at[pl.ds(0, chips * slots - CAP)], give_sem.at[1])

    half_rows = rows_dev // 2
    parts = 4
    piece = half_rows // parts
    sibling = {"narrow": chip * 2 + 1 - core}

    def rows_at(side, p):
        return pl.ds(pl.multiple_of(side * half_rows + p * piece, piece), piece)

    def swap(p):
        return remote(sib_out.at[p], sib_in.at[p], sib_ss.at[p], sib_rs.at[p], sibling)

    def collect(k, p):
        spot = sum_ref.at[chip, rows_at(core, p)]
        return remote(
            spot, spot, col_ss.at[k, p], col_rs.at[k, p], {"narrow": at_chip(k) * 2 + core}
        )

    def pass_on(k, p):
        spot = sum_ref.at[at_chip(chips - k), rows_at(core, p)]
        return remote(spot, spot, pass_ss.at[k, p], pass_rs.at[k, p], sibling)

    for p in range(parts):
        sib_out[p] = mm(hot[rows_at(1 - core, p), :], arriving[...]).astype(BF16)
        swap(p).start()
    for p in range(parts):
        total = mm(hot[rows_at(core, p), :], arriving[...])
        swap(p).wait_recv()
        sum_ref[chip, rows_at(core, p), :] = (total + sib_in[p].astype(F32)).astype(BF16)
        for k in range(1, chips):
            collect(k, p).start()
        pass_on(0, p).start()
    for p in range(parts):
        for k in range(1, chips):
            collect(k, p).wait_recv()
            pass_on(k, p).start()
    for p in range(parts):
        for k in range(chips):
            pass_on(k, p).wait_recv()

    wait_bytes(asks.at[pl.ds(0, n_wide - 1)], ask_sem.at[0])
    wait_bytes(reply.at[pl.ds(0, slots - CAP)], reply_sem.at[0])
    wait_bytes(lanes.at[pl.ds(0, chips - 1)], lane_sem.at[0])
    wait_bytes(outgoing.at[pl.ds(0, chips * slots - CAP)], give_sem.at[0])

    def sent(k):
        peer = lax.rem(me + k, n)
        for step, source in enumerate((qkv_out, heads_out, gatt_out, back_out)):
            wait_bytes(source.at[peer], nss.at[step, peer])

    each(1, n, sent)
    for p in range(parts):
        swap(p).wait_send()
        for k in range(1, chips):
            collect(k, p).wait_send()
        for k in range(chips):
            pass_on(k, p).wait_send()


def run_step(n_wide, n, table, ids, lengths, w_uvqk, w_out, cotangent):
    rows_dev, width = table.shape
    tokens = ids.shape[1]
    att = HEADS * HD
    chips = n // 2
    slots = n_wide * CAP
    cols = width // chips
    parts = 4
    vmem = pl.BlockSpec(memory_space=pltpu.VMEM)
    hbm = pl.BlockSpec(memory_space=pl.ANY)
    dma = pltpu.SemaphoreType.DMA
    return pl.pallas_call(
        functools.partial(step_kernel, n_wide, n),
        out_shape=(
            jax.ShapeDtypeStruct((tokens, width), BF16),
            jax.ShapeDtypeStruct((chips, rows_dev, cols), BF16),
        ),
        in_specs=[hbm, vmem, pl.BlockSpec(memory_space=pltpu.SMEM), hbm, hbm, hbm],
        out_specs=(vmem, vmem),
        scratch_shapes=[
            pltpu.VMEM((rows_dev, width), F32),
            pltpu.VMEM((rows_dev, width), BF16),
            pltpu.VMEM(w_uvqk.shape, BF16),
            pltpu.VMEM(w_out.shape, BF16),
            pltpu.VMEM((tokens, width), BF16),
            pltpu.VMEM((w_uvqk.shape[1], width), BF16),
            pltpu.VMEM((n_wide, 1, 128), jnp.int32),
            pltpu.VMEM((n_wide, 1, 128), jnp.int32),
            pltpu.VMEM((slots, rows_dev), BF16),
            pltpu.VMEM((slots, width), BF16),
            pltpu.VMEM((slots, width), BF16),
            pltpu.VMEM((chips, n_wide // 8, 128), jnp.int32),
            pltpu.VMEM((rows_dev, chips * slots), BF16),
            pltpu.VMEM((tokens, width), F32),
            pltpu.VMEM((4 * att, tokens), F32),
            pltpu.VMEM((width, tokens), F32),
            pltpu.VMEM((n, 3 * HD, tokens), BF16),
            pltpu.VMEM((n, 3 * HD, tokens), BF16),
            pltpu.VMEM((n, tokens, HD), BF16),
            pltpu.VMEM((n, tokens, HD), BF16),
            pltpu.VMEM((n, n, tokens, tokens), BF16),
            pltpu.VMEM((n, n, tokens, tokens), BF16),
            pltpu.VMEM((n, HD, tokens), BF16),
            pltpu.VMEM((n, HD, tokens), BF16),
            pltpu.VMEM((att, tokens), F32),
            pltpu.VMEM((att, tokens), F32),
            pltpu.VMEM((n, HD, tokens), BF16),
            pltpu.VMEM((n, HD, tokens), BF16),
            pltpu.VMEM((8, 128), F32),
            pltpu.VMEM((n, HD, tokens), F32),
            pltpu.VMEM((n, HD, tokens), F32),
            pltpu.VMEM((n, 3 * HD, tokens), BF16),
            pltpu.VMEM((n, 3 * HD, tokens), BF16),
            pltpu.VMEM((4 * att, tokens), BF16),
            pltpu.VMEM((width, tokens), F32),
            pltpu.VMEM((width, tokens), BF16),
            pltpu.VMEM((chips * slots, cols), BF16),
            pltpu.VMEM((chips * slots, cols), BF16),
            pltpu.VMEM((parts, rows_dev // 2 // parts, cols), BF16),
            pltpu.VMEM((parts, rows_dev // 2 // parts, cols), BF16),
            dma((4,)),
            dma((2,)),
            dma((2,)),
            dma((2,)),
            dma((4, n)),
            dma((4, n)),
            dma((2,)),
            dma((parts,)),
            dma((parts,)),
            dma((chips, parts)),
            dma((chips, parts)),
            dma((chips, parts)),
            dma((chips, parts)),
        ],
        compiler_params=pltpu.CompilerParams(
            collective_id=0, has_side_effects=True, vmem_limit_bytes=60 * MIB
        ),
    )(table, ids, lengths, w_uvqk, w_out, cotangent)


def update_kernel(sum_ref, table_ref, accum_ref, out_in, new_table_ref, new_accum_ref, out_out, sem):
    step = pl.program_id(0)
    copy = pltpu.make_async_copy(out_in, out_out, sem)

    @pl.when(step == 0)
    def _():
        copy.start()

    chips, rows, cols = sum_ref.shape
    width = chips * cols
    groups = rows // 128
    for g in range(groups):
        part = slice(g * 128, (g + 1) * 128)
        grads = [sum_ref[y, part, :].astype(F32) for y in range(chips)]
        square = sum(v * v for v in grads)
        mean = jnp.sum(square, axis=1, keepdims=True) * (1.0 / width)
        line = jnp.transpose(jnp.broadcast_to(mean, (128, 128)))[:1, :]
        spot = pl.ds(step * groups + g, 1)
        accum = accum_ref[spot, :] + line
        new_accum_ref[spot, :] = accum
        factor = jnp.transpose(jnp.broadcast_to(RATE * lax.rsqrt(accum), (128, 128)))
        for y in range(chips):
            lane = slice(y * cols, (y + 1) * cols)
            new_table_ref[part, lane] = table_ref[part, lane] - grads[y] * factor

    @pl.when(step == pl.num_programs(0) - 1)
    def _():
        copy.wait()


def update(summed, table, accum, output):
    rows_dev, width = table.shape
    chips, _, cols = summed.shape
    block = min(512, rows_dev)
    whole = pl.BlockSpec((rows_dev // 128, 128), lambda i: (0, 0))
    rows = pl.BlockSpec((block, width), lambda i: (i, 0))
    hbm = pl.BlockSpec(memory_space=pl.ANY)
    new_table, new_accum, result = pl.pallas_call(
        update_kernel,
        grid=(rows_dev // block,),
        out_shape=(
            jax.ShapeDtypeStruct(table.shape, F32),
            jax.ShapeDtypeStruct((rows_dev // 128, 128), F32),
            jax.ShapeDtypeStruct(output.shape, output.dtype),
        ),
        in_specs=[pl.BlockSpec((chips, block, cols), lambda i: (0, i, 0)), rows, whole, hbm],
        out_specs=(rows, whole, hbm),
        scratch_shapes=[pltpu.SemaphoreType.DMA],
        compiler_params=pltpu.CompilerParams(vmem_limit_bytes=24 * MIB),
    )(summed, table, accum.reshape(rows_dev // 128, 128), output)
    return new_table, new_accum.reshape(rows_dev), result


def local(table, accum, ids, lengths, w_uvqk, w_out, cotangent):
    n_wide = lax.axis_size("wide")
    n_narrow = lax.axis_size("narrow")
    width = table.shape[1]
    tokens = ids.shape[1]
    output, summed = run_step(
        n_wide, n_narrow, table, ids, lengths, w_uvqk, w_out, cotangent.reshape(tokens, width)
    )
    new_table, new_accum, output = update(summed, table, accum, output)
    return (output.reshape(1, tokens, width), new_table, new_accum)


def solution(mesh):
    in_specs = (
        P("wide", None),
        P("wide"),
        P("wide", "narrow"),
        P("wide"),
        P(),
        P(),
        P("wide", "narrow", None),
    )
    out_specs = (P("wide", "narrow", None), P("wide", None), P("wide"))
    return jax.shard_map(local, mesh=mesh, in_specs=in_specs, out_specs=out_specs, check_vma=False)
```

time: 380 us -> 120 us (0.32); the launches traced: 373 us -> 120 us
  Pallas kernels: 0 us -> 113 us
  waiting for transfers between devices: 108 us -> 0 us
  other arithmetic: 77.8 us -> 0 us
  blocking collectives: 50 us -> 0 us
  local copies, waits for them, and re-layouts: 53.2 us -> 4.73 us
  matrix products: 46 us -> 0 us
  starting transfers between devices: 22 us -> 0 us
  between operations: 15.3 us -> 1.49 us
    pallas_call x0 -> x2, Pallas kernels: none -> 113 us  [the longest x1 110 us: run_step(): pl.pallas_call(functools.partial(step_kernel, n_wide, n), out_shape=(jax....]
    psum x1 -> x0, waiting for transfers between devices: 63.7 us -> none  [local(): lax.psum(row_grads.astype(jnp.bfloat16), 'narrow').astype(jnp.float32)]
    all_to_all x3 -> x0, blocking collectives: 50 us -> none  [the longest x1 20.2 us: local(): lax.all_to_all(requests, 'wide', split_axis=0, concat_axis=0, tiled=True)]
    dot_general x28 -> x0, matrix products: 46 us -> none  [the longest x4 14.3 us: block_scores(): jnp.einsum('sbhd,skhd->shbk', queries[:, start:start + block], keys_all,...]
    all_to_all x4 -> x0, waiting for transfers between devices: 44.6 us -> none  [the longest x1 14.5 us: local(): lax.all_to_all(fetched, 'wide', split_axis=0, concat_axis=0, tiled=True)]
    unnamed x2 -> x0, other arithmetic: 26.4 us -> none
    all_to_all x4 -> x0, starting transfers between devices: 22 us -> none  [the longest x1 9.2 us: local(): lax.all_to_all(act_rest.reshape(seq_count, stretch, HEADS, 3 * HD), 'narr...]
    reduce_sum x7 -> x0, other arithmetic: 20 us -> none  [the longest x3 16.4 us: layer_norm(): center = value - jnp.mean(value, axis=-1, keepdims=True)]
  transfers between devices with their start and end apart: 5 -> 0, of which waited for: 5 -> 0; matrix products, arithmetic and copies ran while one was open for 1% -> 0% of each run, Pallas kernels for 0% -> 0%
where the time goes in v2:
time: 120 us
  Pallas kernels  113 us (94%)
  local copies, waits for them, and re-layouts  4.73 us (4%)
  between operations  1.49 us (1%)
    pallas_call x1, Pallas kernels, run_step(): pl.pallas_call(functools.partial(step_kernel, n_wide, n), out_shape=(jax....  110 us
    unnamed x8, local copies, waits for them, and re-layouts  4.73 us
    pallas_call x1, Pallas kernels, update(): pl.pallas_call(update_kernel, grid=(rows_dev // block,), out_shape=(jax.S...  3.36 us

profile of v2, /device:TPU:1, one launch (start us, length us, event | category | flops | bytes accessed | tf_op | source)
XLA Modules:
  0.0 119.6 jit_solution(6884185642781336977)
XLA Ops:
  0.6 0.0 copy-start.3
  1.3 110.1 %shard_map.94 = (bf16[256,512]{1,0:T(8,128)(2,1)}, bf16[4,2048,128]{2,1,0:T(8,128)(2,1)}) custom-call(f32[2048,512]{1,0:T(8,128)} %table_ref.3, s32[1,256]{1,0:T(1,128)} %ids_ref.1, s32[1]{0:T(128)S(6)} %copy.10.len_ref, bf16[512,2048]{1,0:T(8,128)(2,1)} %w_hbm.1, bf16[512,512]{1,0:T(8,128)(2,1)} %wo_hbm.1, bf16[256,512]{1,0:T(8,128)(2,1)} %bitcast.5), custom_call_target="tpu_custom_call" | custom-call | tf_op jit(solution)/shard_map/pallas_call | solution.py:445
  111.4 0.0 copy-done.3
  111.4 0.0 copy-start
  111.4 2.2 %copy-done = f32[2048,512]{1,0:T(8,128)S(1)} copy-done((f32[2048,512]{1,0:T(8,128)S(1)}, f32[2048,512]{1,0:T(8,128)}, u32[]{:S(2)}) %copy-start) | copy-done | bytes 4194328
  113.6 0.0 copy-start.1
  113.6 1.6 %copy-done.1 = bf16[4,2048,128]{2,1,0:T(8,128)(2,1)S(1)} copy-done((bf16[4,2048,128]{2,1,0:T(8,128)(2,1)S(1)}, bf16[4,2048,128]{2,1,0:T(8,128)(2,1)}, u32[]{:S(2)}) %copy-start.1) | copy-done | bytes 2097176
  115.2 0.0 copy-start.2
  115.2 0.9 copy-done.2
  116.1 3.4 %shard_map.95 = (f32[2048,512]{1,0:T(8,128)}, f32[16,128]{1,0:T(8,128)}, bf16[256,512]{1,0:T(8,128)(2,1)}) custom-call(bf16[4,2048,128]{2,1,0:T(8,128)(2,1)S(1)} %copy-done.1, f32[2048,512]{1,0:T(8,128)S(1)} %copy-done, f32[16,128]{1,0:T(8,128)S(1)} %bitcast.4, bf16[256,512]{1,0:T(8,128)(2,1)S(1)} %copy-done.2), custom_call_target="tpu_custom_call" | custom-call | tf_op jit(solution)/shard_map/pallas_call | solution.py:551
Async XLA Ops:
  0.6 110.8 %copy-start.3 = (f32[2048]{0:T(1024)S(1)}, f32[2048]{0:T(1024)}, u32[]{:S(2)}) copy-start(f32[2048]{0:T(1024)} %param.8) | copy-start | bytes 24580
  111.4 2.2 %copy-start = (f32[2048,512]{1,0:T(8,128)S(1)}, f32[2048,512]{1,0:T(8,128)}, u32[]{:S(2)}) copy-start(f32[2048,512]{1,0:T(8,128)} %table_ref.3) | copy-start | bytes 12582916
  113.6 1.6 %copy-start.1 = (bf16[4,2048,128]{2,1,0:T(8,128)(2,1)S(1)}, bf16[4,2048,128]{2,1,0:T(8,128)(2,1)}, u32[]{:S(2)}) copy-start(bf16[4,2048,128]{2,1,0:T(8,128)(2,1)} %get-tuple-element.8.sum_ref) | copy-start | bytes 6291460
  115.2 0.9 copy-start.2

commit v3 on v2

v3 whole, which is shorter than its diff:
```python
import functools

import jax
import jax.numpy as jnp
from jax import lax
from jax.experimental import pallas as pl
from jax.experimental.pallas import tpu as pltpu
from jax.sharding import PartitionSpec as P

HEADS = 8
HD = 64
CAP = 16
EPS = 1e-05
RATE = 0.5
MESH = pl.DeviceIdType.MESH
F32 = jnp.float32
BF16 = jnp.bfloat16
MIB = 1 << 20
Z = 8
X = 4
DZ = (4, 3, 5, 2, 6, 1, 7, 0)
DX = (2, 1, 3, 0)
DY = (2, 1, 3, 0)
AROUND = [(dz, dx) for dx in DX for dz in DZ]

NN = (((1,), (0,)), ((), ()))
NT = (((1,), (1,)), ((), ()))
TN = (((0,), (0,)), ((), ()))


def mm(a, b, dims=NN):
    return lax.dot_general(a, b, dims, preferred_element_type=F32)


def iota(shape, dim):
    return lax.broadcasted_iota(jnp.int32, shape, dim)


def sigmoid(t):
    return 0.5 * jnp.tanh(0.5 * t) + 0.5


def silu(t):
    return t * sigmoid(t)


def silu_slope(t):
    s = sigmoid(t)
    return s * (1.0 + t * (1.0 - s))


def norm_back(grad, normed, inverse):
    return inverse * (
        grad
        - jnp.mean(grad, axis=0, keepdims=True)
        - normed * jnp.mean(grad * normed, axis=0, keepdims=True)
    )


def onehot(match):
    return match.astype(F32).astype(BF16)


def each(lower, upper, act):
    def step(k, carry):
        act(k)
        return carry

    lax.fori_loop(lower, upper, step, 0)


def remote(src, dst, send_sem, recv_sem, peer):
    return pltpu.make_async_remote_copy(
        src_ref=src,
        dst_ref=dst,
        send_sem=send_sem,
        recv_sem=recv_sem,
        device_id=peer,
        device_id_type=MESH,
    )


def wait_bytes(ref, sem):
    pltpu.make_async_copy(ref, ref, sem).wait()


def tile16(start):
    return pl.ds(pl.multiple_of(start, CAP), CAP)


def step_kernel(
    n_wide, n, table_ref, accum_ref, ids_ref, len_ref, w_hbm, wo_hbm, cot_hbm,
    out_ref, new_table_ref, new_accum_ref, sum_ref,
    tab, w_ref, wo_ref, cot_ref, wt, asks, asked, reply, replies, lanes, hot,
    emb, hid, normed1, qk_out, qk, v_out, v_in, keys, vals, wts, slopes, heads_out, heads, gm, gu,
    gatt_out, gatt, dk, dv, back_out, back, gh, up_t, ge, outgoing, arriving, sib_out, sib_in,
    load_sem, ask_sem, reply_sem, lane_sem, nss, nrs, give_sem, sib_ss, sib_rs, ring_ss, ring_rs,
    pass_ss, pass_rs,
):
    wide = lax.axis_index("wide")
    me = lax.axis_index("narrow")
    chip = me // 2
    core = lax.rem(me, 2)
    chips = n // 2
    rows_dev, width = table_ref.shape
    tokens = ids_ref.shape[1]
    att = HEADS * HD
    slots = n_wide * CAP
    cols = width // chips

    depth, across = wide // X, lax.rem(wide, X)
    zs = [lax.rem(depth + d, Z) * X for d in range(Z)]
    xs = [lax.rem(across + d, X) for d in range(X)]
    ys = [lax.rem(chip + d, chips) for d in range(chips)]

    def far(dz, dx):
        return zs[dz] + xs[dx]

    finish = []
    barrier = pltpu.get_barrier_semaphore()

    def hail(peer):
        pl.semaphore_signal(barrier, inc=1, device_id=peer, device_id_type=MESH)

    for dz, dx in AROUND:
        for dy in DY:
            if dz or dx or dy:
                hail({"wide": far(dz, dx), "narrow": ys[dy] * 2 + core})
    for dy in DY:
        hail({"wide": wide, "narrow": ys[dy] * 2 + 1 - core})

    loads = [
        pltpu.make_async_copy(src, dst, load_sem.at[i])
        for i, (src, dst) in enumerate(
            ((table_ref, tab), (w_hbm, w_ref), (wo_hbm, wo_ref), (cot_hbm, cot_ref))
        )
    ]
    for load in loads:
        load.start()

    ids = ids_ref[...]
    bits = rows_dev.bit_length() - 1
    owner = lax.shift_right_logical(ids, bits)
    row = ids - owner * rows_dev
    hits_f = (owner == iota((n_wide, tokens), 0)).astype(F32)
    before = onehot(iota((tokens, tokens), 0) < iota((tokens, tokens), 1))
    earlier = mm(hits_f.astype(BF16), before)
    slot = jnp.sum(earlier * hits_f, axis=0, keepdims=True).astype(jnp.int32)
    target = owner * CAP + slot
    place = slot + CAP * lax.rem(wide, 8)
    at_place = onehot(place == iota((128, tokens), 0))
    high = lax.shift_right_logical(row, 8)
    low = row - high * 256
    high_m = (hits_f * high.astype(F32)).astype(BF16)
    low_m = (hits_f * low.astype(F32)).astype(BF16)
    wanted = (mm(high_m, at_place, NT) * 256.0 + mm(low_m, at_place, NT)).astype(jnp.int32)
    for o in range(n_wide):
        asks[o] = wanted[o : o + 1, :]

    pl.semaphore_wait(barrier, n_wide * chips - 1 + chips)

    for dz, dx in AROUND[:-1]:
        peer = far(dz, dx)
        remote(
            asks.at[peer], asked.at[wide], ask_sem.at[0], ask_sem.at[1], {"wide": peer}
        ).start()
    finish.append(lambda: wait_bytes(asks.at[pl.ds(0, n_wide - 1)], ask_sem.at[0]))
    asked[wide] = asks[wide]
    loads[0].wait()
    wt[...] = tab[...].astype(BF16)
    wait_bytes(asked.at[pl.ds(0, n_wide - 1)], ask_sem.at[1])

    lane16 = iota((CAP, 128), 1)
    sub16 = iota((CAP, 128), 0)
    row_iota = iota((CAP, rows_dev), 1)

    half = n_wide // 2
    for part in range(2):
        for k in range(part * half, (part + 1) * half):
            peer = far(*AROUND[k])
            line = jnp.broadcast_to(asked[peer], (CAP, 128)).astype(F32)
            mine = lane16 == sub16 + CAP * lax.rem(peer, 8)
            column = jnp.sum(jnp.where(mine, line, 0.0), axis=1, keepdims=True).astype(jnp.int32)
            hot[CAP * k : CAP * (k + 1), :] = onehot(column == row_iota)
        lo = part * half * CAP
        reply[lo : lo + half * CAP, :] = mm(hot[lo : lo + half * CAP, :], wt[...]).astype(BF16)
        for k in range(part * half, min((part + 1) * half, n_wide - 1)):
            remote(
                reply.at[pl.ds(k * CAP, CAP)],
                replies.at[tile16(wide * CAP)],
                reply_sem.at[0],
                reply_sem.at[1],
                {"wide": far(*AROUND[k])},
            ).start()
    replies[tile16(wide * CAP), :] = reply[slots - CAP :, :]
    finish.append(lambda: wait_bytes(reply.at[pl.ds(0, slots - CAP)], reply_sem.at[0]))

    for g in range(n_wide // 8):
        total = asked[8 * g]
        for j in range(1, 8):
            total = total + asked[8 * g + j]
        lanes[chip, g : g + 1, :] = total
    for k in range(1, chips):
        remote(
            lanes.at[chip], lanes.at[chip], lane_sem.at[0], lane_sem.at[1],
            {"narrow": ys[k] * 2 + core},
        ).start()
    finish.append(lambda: wait_bytes(lanes.at[pl.ds(0, chips - 1)], lane_sem.at[0]))

    target_t = jnp.transpose(jnp.broadcast_to(target.astype(F32), (128, tokens))).astype(jnp.int32)
    take = jnp.concatenate(
        [onehot(target_t == iota((tokens, 128), 1) + 128 * g) for g in range(slots // 128)],
        axis=1,
    )

    length = len_ref[0]
    live = iota((tokens, 1), 0) + me * tokens < length
    live_t = iota((1, tokens), 1) + me * tokens < length
    for load in loads[1:]:
        load.wait()
    chunk = 256
    eye = onehot(iota((chunk, chunk), 0) == iota((chunk, chunk), 1))
    total_w = w_ref.shape[1]
    for c in range(total_w // chunk):
        part = slice(c * chunk, (c + 1) * chunk)
        wt[part, :] = mm(eye, w_ref[:, part], NT).astype(BF16)
    upstream = jnp.where(live, cot_ref[...], jnp.zeros((), BF16))
    gm[...] = mm(wo_ref[...], upstream, NT)
    up_t[...] = jnp.transpose(upstream.astype(F32))
    wait_bytes(lanes.at[pl.ds(0, chips - 1)], lane_sem.at[1])
    for y in range(chips):
        for g in range(slots // 128):
            lo = y * slots + 128 * g
            hot[:, lo : lo + 128] = onehot(iota((rows_dev, 128), 0) == lanes[y, g : g + 1, :])
    wait_bytes(replies.at[pl.ds(0, slots - CAP)], reply_sem.at[1])
    emb[...] = mm(take, replies[...])

    def exchange(step, source, landing, peer):
        return remote(
            source.at[peer],
            landing.at[me],
            nss.at[step, peer],
            nrs.at[step, me],
            {"narrow": peer},
        )

    def arrive(step, landing, peer):
        wait_bytes(landing.at[peer], nrs.at[step, peer])

    def sent(step, source):
        def one(k):
            peer = lax.rem(me + k, n)
            wait_bytes(source.at[peer], nss.at[step, peer])

        return lambda: each(1, n, one)

    emb_t = jnp.transpose(emb[...])
    center = emb_t - jnp.mean(emb_t, axis=0, keepdims=True)
    inverse1 = lax.rsqrt(jnp.mean(center * center, axis=0, keepdims=True) + EPS)
    normed = center * inverse1
    normed1[...] = normed
    normed_b = normed.astype(BF16)
    for c in range(att // chunk, total_w // chunk):
        hid[c * chunk : (c + 1) * chunk, :] = mm(wt[c * chunk : (c + 1) * chunk, :], normed_b)

    def send_head(k):
        peer = lax.rem(me + k, n)
        base = pl.multiple_of(att + 3 * HD * peer, HD)
        qk_out[peer] = silu(hid[pl.ds(base + HD, 2 * HD), :]).astype(BF16)
        exchange(0, qk_out, qk, peer).start()

    def send_values(k):
        peer = lax.rem(me + k, n)
        base = pl.multiple_of(att + 3 * HD * peer, HD)
        v_out[peer] = hid[pl.ds(base, HD), :].astype(BF16)
        exchange(4, v_out, v_in, peer).start()

    each(1, n, send_head)
    each(1, n, send_values)
    finish.append(sent(0, qk_out))
    finish.append(sent(4, v_out))
    base = pl.multiple_of(att + 3 * HD * me, HD)
    qk[me] = silu(hid[pl.ds(base + HD, 2 * HD), :]).astype(BF16)
    v_in[me] = hid[pl.ds(base, HD), :].astype(BF16)

    for c in range(att // chunk):
        hid[c * chunk : (c + 1) * chunk, :] = mm(wt[c * chunk : (c + 1) * chunk, :], normed_b)
    each(1, n, lambda k: arrive(0, qk, lax.rem(me + k, n)))

    scale = HD**-0.5
    for b in range(n):
        keys[b] = jnp.transpose(qk[b, HD:, :].astype(F32)).astype(BF16)
    causal = iota((tokens, tokens), 0) <= iota((tokens, tokens), 1)

    def tri(j, i):
        return i * (i + 1) // 2 + j

    def weigh(j, i, query):
        score = mm(keys[j], query)
        twice = 1.0 + jnp.tanh(score)
        weight = score * twice
        slope = twice + weight * (2.0 - twice)
        if i == j:
            weight = jnp.where(causal, weight, 0.0)
            slope = jnp.where(causal, slope, 0.0)
        weight = weight.astype(BF16)
        wts[tri(j, i)] = weight
        slopes[tri(j, i)] = slope.astype(BF16)
        return weight

    def send_block(step, source, landing, i):
        @pl.when(i != me)
        def _():
            exchange(step, source, landing, i).start()

        @pl.when(i == me)
        def _():
            landing[i] = source[i]

    early = 2
    for i in range(n - 1, n - 1 - early, -1):
        query = qk[i, :HD, :] * (0.5 * scale)
        for j in range(i + 1):
            weigh(j, i, query)
    each(1, n, lambda k: arrive(4, v_in, lax.rem(me + k, n)))
    for i in reversed(range(n)):
        query = qk[i, :HD, :] * (0.5 * scale)
        attended = jnp.zeros((HD, tokens), F32)
        for j in range(i + 1):
            weight = weigh(j, i, query) if i < n - early else wts[tri(j, i)]
            attended = attended + mm(v_in[j], weight)
        heads_out[i] = attended.astype(BF16)
        send_block(1, heads_out, heads, i)
    for b in range(n):
        vals[b] = jnp.transpose(v_in[b].astype(F32)).astype(BF16)

    finish.append(sent(1, heads_out))
    each(1, n, lambda k: arrive(1, heads, lax.rem(me + k, n)))

    merged = heads[...].astype(F32).reshape(att, tokens)
    center = merged - jnp.mean(merged, axis=0, keepdims=True)
    inverse2 = lax.rsqrt(jnp.mean(center * center, axis=0, keepdims=True) + EPS)
    normed2 = center * inverse2
    gate = silu(hid[:att, :]).astype(BF16).astype(F32)
    grad_mixed = gm[...]
    gu[...] = grad_mixed * normed2
    grad_att = norm_back(grad_mixed * gate, normed2, inverse2).astype(BF16)
    gatt_out[...] = grad_att.reshape(n, HD, tokens)
    each(1, n, lambda k: exchange(2, gatt_out, gatt, lax.rem(me + k, n)).start())
    finish.append(sent(2, gatt_out))
    gatt[me] = gatt_out[me]
    mixed = jnp.transpose(normed2 * gate).astype(BF16)
    result = emb[...] + mm(mixed, wo_ref[...])
    out_ref[...] = jnp.where(live, result, 0.0).astype(BF16)
    gh[:att, :] = (gu[...] * silu_slope(hid[:att, :])).astype(BF16)
    dk[...] = jnp.zeros_like(dk)
    dv[...] = jnp.zeros_like(dv)

    for i in reversed(range(n)):

        @pl.when(i != me)
        def _():
            arrive(2, gatt, i)

        grad = gatt[i]
        query = qk[i, :HD, :]
        dq = jnp.zeros((HD, tokens), F32)
        for j in range(i + 1):
            dw = mm(vals[j], grad)
            ds = (dw * slopes[tri(j, i)].astype(F32)).astype(BF16)
            dv[j] += mm(grad, wts[tri(j, i)], NT)
            dk[j] += mm(query, ds, NT)
            dq = dq + mm(qk[j, HD:, :], ds)
        back_out[i, :HD, :] = dv[i].astype(BF16)
        back_out[i, HD : 2 * HD, :] = (dq * (0.5 * scale)).astype(BF16)
        back_out[i, 2 * HD :, :] = (dk[i] * (0.5 * scale)).astype(BF16)
        send_block(3, back_out, back, i)

    finish.append(sent(3, back_out))
    hid[att:, :] = silu_slope(hid[att:, :])
    put = onehot(iota((slots, tokens), 0) == target)
    each(1, n, lambda k: arrive(3, back, lax.rem(me + k, n)))
    for h in range(HEADS):
        base = att + 3 * HD * h
        gh[base : base + HD, :] = back[h, :HD, :]
        gh[base + HD : base + 3 * HD, :] = (
            back[h, HD:, :].astype(F32) * hid[base + HD : base + 3 * HD, :]
        ).astype(BF16)
    grad_norm1 = mm(w_ref[...], gh[...])
    grad_emb = norm_back(grad_norm1, normed1[...], inverse1) + up_t[...]
    ge[...] = jnp.where(live_t, grad_emb, 0.0).astype(BF16)

    own = tile16(chip * slots + wide * CAP)

    for dy in DY:
        y = ys[dy]
        block = ge[pl.ds(pl.multiple_of(y * cols, cols), cols), :]
        outgoing[pl.ds(pl.multiple_of(y * slots, slots), slots), :] = mm(put, block, NT).astype(BF16)
        for dz, dx in AROUND:
            if dz or dx or dy:
                o = far(dz, dx)
                remote(
                    outgoing.at[tile16(y * slots + o * CAP)],
                    arriving.at[own],
                    give_sem.at[0],
                    give_sem.at[1],
                    {"wide": o, "narrow": y * 2 + core},
                ).start()
    finish.append(lambda: wait_bytes(outgoing.at[pl.ds(0, chips * slots - CAP)], give_sem.at[0]))
    arriving[own, :] = outgoing[own, :]
    wait_bytes(arriving.at[pl.ds(0, chips * slots - CAP)], give_sem.at[1])

    half_rows = rows_dev // 2
    parts = 4
    piece = half_rows // parts
    sibling = {"narrow": chip * 2 + 1 - core}

    def rows_at(side, p):
        return pl.ds(pl.multiple_of(side * half_rows + p * piece, piece), piece)

    def swap(p):
        return remote(sib_out.at[p], sib_in.at[p], sib_ss.at[p], sib_rs.at[p], sibling)

    def ring(way, hop, p):
        spot = sum_ref.at[ys[(1 - hop) * way % chips], rows_at(core, p)]
        lane = 2 * hop - 2 + (way < 0)
        return remote(
            spot, spot, ring_ss.at[lane, p], ring_rs.at[lane, p], {"narrow": ys[way % chips] * 2 + core}
        )

    def pass_on(k, p):
        spot = sum_ref.at[ys[k], rows_at(core, p)]
        return remote(spot, spot, pass_ss.at[k, p], pass_rs.at[k, p], sibling)

    groups = piece // 128

    def update(side, p):
        first = side * (half_rows // 128) + p * groups
        for g in range(groups):
            part = pl.ds(pl.multiple_of(side * half_rows + p * piece + g * 128, 128), 128)
            grads = [sum_ref[y, part, :].astype(F32) for y in range(chips)]
            square = sum(v * v for v in grads)
            mean = jnp.sum(square, axis=1, keepdims=True) * (1.0 / width)
            line = jnp.transpose(jnp.broadcast_to(mean, (128, 128)))[:1, :]
            spot = pl.ds(first + g, 1)
            accum = accum_ref[spot, :] + line
            new_accum_ref[spot, :] = accum
            factor = jnp.transpose(jnp.broadcast_to(RATE * lax.rsqrt(accum), (128, 128)))
            for y in range(chips):
                lane = slice(y * cols, (y + 1) * cols)
                new_table_ref[part, lane] = tab[part, lane] - grads[y] * factor

    low, high = tuple(range(parts // 2)), tuple(range(parts // 2, parts))
    order = [p for pair in zip(low, high) for p in pair]
    for p in order:
        sib_out[p] = mm(hot[rows_at(1 - core, p), :], arriving[...]).astype(BF16)
        swap(p).start()
    for p in order:
        total = mm(hot[rows_at(core, p), :], arriving[...])
        swap(p).wait_recv()
        sum_ref[chip, rows_at(core, p), :] = (total + sib_in[p].astype(F32)).astype(BF16)
        ring(1 if p in low else -1, 1, p).start()
        pass_on(0, p).start()
    for p in order:
        ring(-1 if p in low else 1, 1, p).start()
    for p in order:
        way = 1 if p in low else -1
        ring(way, 1, p).wait_recv()
        ring(way, 2, p).start()
        pass_on(-way % chips, p).start()
    for at, p in enumerate(order):
        way = 1 if p in low else -1
        ring(-way, 1, p).wait_recv()
        pass_on(way % chips, p).start()
    for at, p in enumerate(order):
        way = 1 if p in low else -1
        ring(way, 2, p).wait_recv()
        pass_on(2, p).start()
        update(core, p)
        if at:
            q = order[at - 1]
            for k in range(chips):
                pass_on(k, q).wait_recv()
            update(1 - core, q)
    for k in range(chips):
        pass_on(k, order[-1]).wait_recv()
    update(1 - core, order[-1])

    for wait in finish:
        wait()
    for p in range(parts):
        swap(p).wait_send()
        for way in (1, -1):
            ring(way, 1, p).wait_send()
        ring(1 if p in low else -1, 2, p).wait_send()
        for k in range(chips):
            pass_on(k, p).wait_send()


def run_step(n_wide, n, table, accum, ids, lengths, w_uvqk, w_out, cotangent):
    rows_dev, width = table.shape
    tokens = ids.shape[1]
    att = HEADS * HD
    chips = n // 2
    slots = n_wide * CAP
    cols = width // chips
    parts = 4
    vmem = pl.BlockSpec(memory_space=pltpu.VMEM)
    hbm = pl.BlockSpec(memory_space=pltpu.HBM)
    dma = pltpu.SemaphoreType.DMA
    return pl.pallas_call(
        functools.partial(step_kernel, n_wide, n),
        out_shape=(
            pltpu.VMEM((tokens, width), BF16),
            pltpu.VMEM((rows_dev, width), F32),
            pltpu.VMEM((rows_dev // 128, 128), F32),
        ),
        in_specs=[hbm, vmem, vmem, pl.BlockSpec(memory_space=pltpu.SMEM), hbm, hbm, hbm],
        out_specs=(vmem, vmem, vmem),
        scratch_shapes=[
            pltpu.VMEM((chips, rows_dev, cols), BF16),
            pltpu.VMEM((rows_dev, width), F32),
            pltpu.VMEM(w_uvqk.shape, BF16),
            pltpu.VMEM(w_out.shape, BF16),
            pltpu.VMEM((tokens, width), BF16),
            pltpu.VMEM((w_uvqk.shape[1], width), BF16),
            pltpu.VMEM((n_wide, 1, 128), jnp.int32),
            pltpu.VMEM((n_wide, 1, 128), jnp.int32),
            pltpu.VMEM((slots, width), BF16),
            pltpu.VMEM((slots, width), BF16),
            pltpu.VMEM((chips, n_wide // 8, 128), jnp.int32),
            pltpu.VMEM((rows_dev, chips * slots), BF16),
            pltpu.VMEM((tokens, width), F32),
            pltpu.VMEM((4 * att, tokens), F32),
            pltpu.VMEM((width, tokens), F32),
            pltpu.VMEM((n, 2 * HD, tokens), BF16),
            pltpu.VMEM((n, 2 * HD, tokens), BF16),
            pltpu.VMEM((n, HD, tokens), BF16),
            pltpu.VMEM((n, HD, tokens), BF16),
            pltpu.VMEM((n, tokens, HD), BF16),
            pltpu.VMEM((n, tokens, HD), BF16),
            pltpu.VMEM((n * (n + 1) // 2, tokens, tokens), BF16),
            pltpu.VMEM((n * (n + 1) // 2, tokens, tokens), BF16),
            pltpu.VMEM((n, HD, tokens), BF16),
            pltpu.VMEM((n, HD, tokens), BF16),
            pltpu.VMEM((att, tokens), F32),
            pltpu.VMEM((att, tokens), F32),
            pltpu.VMEM((n, HD, tokens), BF16),
            pltpu.VMEM((n, HD, tokens), BF16),
            pltpu.VMEM((n, HD, tokens), F32),
            pltpu.VMEM((n, HD, tokens), F32),
            pltpu.VMEM((n, 3 * HD, tokens), BF16),
            pltpu.VMEM((n, 3 * HD, tokens), BF16),
            pltpu.VMEM((4 * att, tokens), BF16),
            pltpu.VMEM((width, tokens), F32),
            pltpu.VMEM((width, tokens), BF16),
            pltpu.VMEM((chips * slots, cols), BF16),
            pltpu.VMEM((chips * slots, cols), BF16),
            pltpu.VMEM((parts, rows_dev // 2 // parts, cols), BF16),
            pltpu.VMEM((parts, rows_dev // 2 // parts, cols), BF16),
            dma((4,)),
            dma((2,)),
            dma((2,)),
            dma((2,)),
            dma((5, n)),
            dma((5, n)),
            dma((2,)),
            dma((parts,)),
            dma((parts,)),
            dma((4, parts)),
            dma((4, parts)),
            dma((chips, parts)),
            dma((chips, parts)),
        ],
        compiler_params=pltpu.CompilerParams(
            collective_id=0, has_side_effects=True, vmem_limit_bytes=52 * MIB
        ),
    )(table, accum, ids, lengths, w_uvqk, w_out, cotangent)


def local(table, accum, ids, lengths, w_uvqk, w_out, cotangent):
    n_wide = lax.axis_size("wide")
    n_narrow = lax.axis_size("narrow")
    width = table.shape[1]
    tokens = ids.shape[1]
    output, new_table, new_accum = run_step(
        n_wide,
        n_narrow,
        table,
        accum.reshape(-1, 128),
        ids,
        lengths,
        w_uvqk,
        w_out,
        cotangent.reshape(tokens, width),
    )
    return (output.reshape(1, tokens, width), new_table, new_accum.reshape(accum.shape))


def solution(mesh):
    in_specs = (
        P("wide", None),
        P("wide"),
        P("wide", "narrow"),
        P("wide"),
        P(),
        P(),
        P("wide", "narrow", None),
    )
    out_specs = (P("wide", "narrow", None), P("wide", None), P("wide"))
    return jax.shard_map(local, mesh=mesh, in_specs=in_specs, out_specs=out_specs, check_vma=False)
```

time: 120 us -> 106 us (0.88)
  Pallas kernels: 113 us -> 101 us
  local copies, waits for them, and re-layouts: 4.73 us -> 3.32 us
    pallas_call x2 -> x1, Pallas kernels: 113 us -> 101 us  [run_step(): pl.pallas_call(functools.partial(step_kernel, n_wide, n), out_shape=(pltp...]
    unnamed x8 -> x3, local copies, waits for them, and re-layouts: 4.73 us -> 3.32 us
where the time goes in v3:
time: 106 us
  Pallas kernels  101 us (95%)
  local copies, waits for them, and re-layouts  3.32 us (3%)
  between operations  1.29 us (1%)
    pallas_call x1, Pallas kernels, run_step(): pl.pallas_call(functools.partial(step_kernel, n_wide, n), out_shape=(pltp...  101 us
    unnamed x3, local copies, waits for them, and re-layouts  3.32 us

profile of v3, /device:TPU:1, one launch (start us, length us, event | category | flops | bytes accessed | tf_op | source)
XLA Modules:
  0.0 106.0 jit_solution(5387797043005373842)
XLA Ops:
  1.3 101.4 %shard_map.94 = (bf16[256,512]{1,0:T(8,128)(2,1)S(1)}, f32[2048,512]{1,0:T(8,128)S(1)}, f32[16,128]{1,0:T(8,128)S(1)}) custom-call(f32[2048,512]{1,0:T(8,128)} %table_ref.1, f32[16,128]{1,0:T(8,128)} %bitcast.7, s32[1,256]{1,0:T(1,128)} %ids_ref.1, s32[1]{0:T(128)S(6)} %copy.16.len_ref, bf16[512,2048]{1,0:T(8,128)(2,1)} %w_hbm.1, bf16[512,512]{1,0:T(8,128)(2,1)} %wo_hbm.1, ...), custom_call_target="tpu_custom_call" | custom-call | tf_op jit(solution)/shard_map/pallas_call | solution.py:511
  102.7 0.7 copy.13
  103.4 0.6 copy.15
  104.0 2.0 %copy.14 = f32[2048,512]{1,0:T(8,128)} copy(f32[2048,512]{1,0:T(8,128)S(1)} %get-tuple-element.10) | data formatting | bytes 8388608

commit v4 on v3

--- a/solution.py
+++ b/solution.py
@@ -116,19 +116,6 @@
     def far(dz, dx):
         return zs[dz] + xs[dx]
 
-    finish = []
-    barrier = pltpu.get_barrier_semaphore()
-
-    def hail(peer):
-        pl.semaphore_signal(barrier, inc=1, device_id=peer, device_id_type=MESH)
-
-    for dz, dx in AROUND:
-        for dy in DY:
-            if dz or dx or dy:
-                hail({"wide": far(dz, dx), "narrow": ys[dy] * 2 + core})
-    for dy in DY:
-        hail({"wide": wide, "narrow": ys[dy] * 2 + 1 - core})
-
     loads = [
         pltpu.make_async_copy(src, dst, load_sem.at[i])
         for i, (src, dst) in enumerate(
@@ -137,6 +124,17 @@
     ]
     for load in loads:
         load.start()
+
+    finish = []
+    barrier = pltpu.get_barrier_semaphore()
+
+    def hail(peer):
+        pl.semaphore_signal(barrier, inc=1, device_id=peer, device_id_type=MESH)
+
+    for dz, dx in AROUND[:-1]:
+        hail({"wide": far(dz, dx)})
+    for k in range(1, n):
+        hail({"narrow": lax.rem(me + k, n)})
 
     ids = ids_ref[...]
     bits = rows_dev.bit_length() - 1
@@ -157,7 +155,7 @@
     for o in range(n_wide):
         asks[o] = wanted[o : o + 1, :]
 
-    pl.semaphore_wait(barrier, n_wide * chips - 1 + chips)
+    pl.semaphore_wait(barrier, n_wide - 1 + n - 1)
 
     for dz, dx in AROUND[:-1]:
         peer = far(dz, dx)
@@ -174,8 +172,8 @@
     sub16 = iota((CAP, 128), 0)
     row_iota = iota((CAP, rows_dev), 1)
 
-    half = n_wide // 2
-    for part in range(2):
+    half = n_wide // 4
+    for part in range(4):
         for k in range(part * half, (part + 1) * half):
             peer = far(*AROUND[k])
             line = jnp.broadcast_to(asked[peer], (CAP, 128)).astype(F32)
@@ -317,7 +315,7 @@
         def _():
             landing[i] = source[i]
 
-    early = 2
+    early = 3
     for i in range(n - 1, n - 1 - early, -1):
         query = qk[i, :HD, :] * (0.5 * scale)
         for j in range(i + 1):
@@ -452,10 +450,15 @@
 
     low, high = tuple(range(parts // 2)), tuple(range(parts // 2, parts))
     order = [p for pair in zip(low, high) for p in pair]
-    for p in order:
+
+    def offer(p):
         sib_out[p] = mm(hot[rows_at(1 - core, p), :], arriving[...]).astype(BF16)
         swap(p).start()
-    for p in order:
+
+    offer(order[0])
+    for at, p in enumerate(order):
+        if at + 1 < parts:
+            offer(order[at + 1])
         total = mm(hot[rows_at(core, p), :], arriving[...])
         swap(p).wait_recv()
         sum_ref[chip, rows_at(core, p), :] = (total + sib_in[p].astype(F32)).astype(BF16)

time: 106 us -> 104 us (0.981)
  Pallas kernels: 101 us -> 99 us
    pallas_call x1, Pallas kernels: 101 us -> 99 us  [run_step(): pl.pallas_call(functools.partial(step_kernel, n_wide, n), out_shape=(pltp...]
where the time goes in v4:
time: 104 us
  Pallas kernels  99 us (95%)
  local copies, waits for them, and re-layouts  3.32 us (3%)
  between operations  1.29 us (1%)
    pallas_call x1, Pallas kernels, run_step(): pl.pallas_call(functools.partial(step_kernel, n_wide, n), out_shape=(pltp...  99 us
    unnamed x3, local copies, waits for them, and re-layouts  3.32 us

profile of v4, /device:TPU:1, one launch (start us, length us, event | category | flops | bytes accessed | tf_op | source)
XLA Modules:
  0.0 103.6 jit_solution(4269522403576518933)
XLA Ops:
  1.3 99.0 %shard_map.94 = (bf16[256,512]{1,0:T(8,128)(2,1)S(1)}, f32[2048,512]{1,0:T(8,128)S(1)}, f32[16,128]{1,0:T(8,128)S(1)}) custom-call(f32[2048,512]{1,0:T(8,128)} %table_ref.1, f32[16,128]{1,0:T(8,128)} %bitcast.7, s32[1,256]{1,0:T(1,128)} %ids_ref.1, s32[1]{0:T(128)S(6)} %copy.16.len_ref, bf16[512,2048]{1,0:T(8,128)(2,1)} %w_hbm.1, bf16[512,512]{1,0:T(8,128)(2,1)} %wo_hbm.1, ...), custom_call_target="tpu_custom_call" | custom-call | tf_op jit(solution)/shard_map/pallas_call | solution.py:514
  100.3 0.7 copy.13
  101.0 0.6 copy.15
  101.6 2.0 %copy.14 = f32[2048,512]{1,0:T(8,128)} copy(f32[2048,512]{1,0:T(8,128)S(1)} %get-tuple-element.10) | data formatting | bytes 8388608

commit v5 on v4

--- a/solution.py
+++ b/solution.py
@@ -92,7 +92,7 @@
     n_wide, n, table_ref, accum_ref, ids_ref, len_ref, w_hbm, wo_hbm, cot_hbm,
     out_ref, new_table_ref, new_accum_ref, sum_ref,
     tab, w_ref, wo_ref, cot_ref, wt, asks, asked, reply, replies, lanes, hot,
-    emb, hid, normed1, qk_out, qk, v_out, v_in, keys, vals, wts, slopes, heads_out, heads, gm, gu,
+    emb, hid, normed1, qk_out, qk, v_out, v_in, keys, vals, wts, slopes, heads_out, heads, gm, gu, gates, gn,
     gatt_out, gatt, dk, dv, back_out, back, gh, up_t, ge, outgoing, arriving, sib_out, sib_in,
     load_sem, ask_sem, reply_sem, lane_sem, nss, nrs, give_sem, sib_ss, sib_rs, ring_ss, ring_rs,
     pass_ss, pass_rs,
@@ -261,20 +261,18 @@
     for c in range(att // chunk, total_w // chunk):
         hid[c * chunk : (c + 1) * chunk, :] = mm(wt[c * chunk : (c + 1) * chunk, :], normed_b)
 
-    def send_head(k):
-        peer = lax.rem(me + k, n)
+    near = [me, chip * 2 + 1 - core]
+    near += [ys[dy] * 2 + c for dy in (1, 3) for c in (core, 1 - core)]
+    near += [ys[2] * 2 + c for c in (core, 1 - core)]
+
+    for peer in near[1:]:
         base = pl.multiple_of(att + 3 * HD * peer, HD)
         qk_out[peer] = silu(hid[pl.ds(base + HD, 2 * HD), :]).astype(BF16)
         exchange(0, qk_out, qk, peer).start()
-
-    def send_values(k):
-        peer = lax.rem(me + k, n)
+    for peer in near[1:]:
         base = pl.multiple_of(att + 3 * HD * peer, HD)
         v_out[peer] = hid[pl.ds(base, HD), :].astype(BF16)
         exchange(4, v_out, v_in, peer).start()
-
-    each(1, n, send_head)
-    each(1, n, send_values)
     finish.append(sent(0, qk_out))
     finish.append(sent(4, v_out))
     base = pl.multiple_of(att + 3 * HD * me, HD)
@@ -283,28 +281,36 @@
 
     for c in range(att // chunk):
         hid[c * chunk : (c + 1) * chunk, :] = mm(wt[c * chunk : (c + 1) * chunk, :], normed_b)
-    each(1, n, lambda k: arrive(0, qk, lax.rem(me + k, n)))
+    gate = hid[:att, :]
+    gates[...] = silu(gate).astype(BF16).astype(F32)
+    gn[...] = gm[...] * gates[...]
+    gu[...] = silu_slope(gate)
 
     scale = HD**-0.5
-    for b in range(n):
-        keys[b] = jnp.transpose(qk[b, HD:, :].astype(F32)).astype(BF16)
     causal = iota((tokens, tokens), 0) <= iota((tokens, tokens), 1)
 
     def tri(j, i):
         return i * (i + 1) // 2 + j
 
-    def weigh(j, i, query):
-        score = mm(keys[j], query)
+    def weigh(j, i, diagonal):
+        score = mm(keys[j], qk[i, :HD, :] * (0.5 * scale))
         twice = 1.0 + jnp.tanh(score)
         weight = score * twice
         slope = twice + weight * (2.0 - twice)
-        if i == j:
+        if diagonal:
             weight = jnp.where(causal, weight, 0.0)
             slope = jnp.where(causal, slope, 0.0)
-        weight = weight.astype(BF16)
-        wts[tri(j, i)] = weight
+        wts[tri(j, i)] = weight.astype(BF16)
         slopes[tri(j, i)] = slope.astype(BF16)
-        return weight
+
+    for at, here in enumerate(near):
+        if at:
+            arrive(0, qk, here)
+        keys[here] = jnp.transpose(qk[here, HD:, :].astype(F32)).astype(BF16)
+        for other in near[:at]:
+            later = (here + n - other) // n
+            weigh(here + later * (other - here), other + later * (here - other), False)
+        weigh(here, here, True)
 
     def send_block(step, source, landing, i):
         @pl.when(i != me)
@@ -315,18 +321,11 @@
         def _():
             landing[i] = source[i]
 
-    early = 3
-    for i in range(n - 1, n - 1 - early, -1):
-        query = qk[i, :HD, :] * (0.5 * scale)
-        for j in range(i + 1):
-            weigh(j, i, query)
     each(1, n, lambda k: arrive(4, v_in, lax.rem(me + k, n)))
     for i in reversed(range(n)):
-        query = qk[i, :HD, :] * (0.5 * scale)
         attended = jnp.zeros((HD, tokens), F32)
         for j in range(i + 1):
-            weight = weigh(j, i, query) if i < n - early else wts[tri(j, i)]
-            attended = attended + mm(v_in[j], weight)
+            attended = attended + mm(v_in[j], wts[tri(j, i)])
         heads_out[i] = attended.astype(BF16)
         send_block(1, heads_out, heads, i)
     for b in range(n):
@@ -339,18 +338,15 @@
     center = merged - jnp.mean(merged, axis=0, keepdims=True)
     inverse2 = lax.rsqrt(jnp.mean(center * center, axis=0, keepdims=True) + EPS)
     normed2 = center * inverse2
-    gate = silu(hid[:att, :]).astype(BF16).astype(F32)
-    grad_mixed = gm[...]
-    gu[...] = grad_mixed * normed2
-    grad_att = norm_back(grad_mixed * gate, normed2, inverse2).astype(BF16)
+    grad_att = norm_back(gn[...], normed2, inverse2).astype(BF16)
     gatt_out[...] = grad_att.reshape(n, HD, tokens)
     each(1, n, lambda k: exchange(2, gatt_out, gatt, lax.rem(me + k, n)).start())
     finish.append(sent(2, gatt_out))
     gatt[me] = gatt_out[me]
-    mixed = jnp.transpose(normed2 * gate).astype(BF16)
+    mixed = jnp.transpose(normed2 * gates[...]).astype(BF16)
     result = emb[...] + mm(mixed, wo_ref[...])
     out_ref[...] = jnp.where(live, result, 0.0).astype(BF16)
-    gh[:att, :] = (gu[...] * silu_slope(hid[:att, :])).astype(BF16)
+    gh[:att, :] = (gm[...] * normed2 * gu[...]).astype(BF16)
     dk[...] = jnp.zeros_like(dk)
     dv[...] = jnp.zeros_like(dv)
 
@@ -377,6 +373,7 @@
     finish.append(sent(3, back_out))
     hid[att:, :] = silu_slope(hid[att:, :])
     put = onehot(iota((slots, tokens), 0) == target)
+    gate_part = mm(w_ref[:, :att], gh[:att, :])
     each(1, n, lambda k: arrive(3, back, lax.rem(me + k, n)))
     for h in range(HEADS):
         base = att + 3 * HD * h
@@ -384,7 +381,7 @@
         gh[base + HD : base + 3 * HD, :] = (
             back[h, HD:, :].astype(F32) * hid[base + HD : base + 3 * HD, :]
         ).astype(BF16)
-    grad_norm1 = mm(w_ref[...], gh[...])
+    grad_norm1 = gate_part + mm(w_ref[:, att:], gh[att:, :])
     grad_emb = norm_back(grad_norm1, normed1[...], inverse1) + up_t[...]
     ge[...] = jnp.where(live_t, grad_emb, 0.0).astype(BF16)
 
@@ -548,6 +545,8 @@
             pltpu.VMEM((n, HD, tokens), BF16),
             pltpu.VMEM((att, tokens), F32),
             pltpu.VMEM((att, tokens), F32),
+            pltpu.VMEM((att, tokens), F32),
+            pltpu.VMEM((att, tokens), F32),
             pltpu.VMEM((n, HD, tokens), BF16),
             pltpu.VMEM((n, HD, tokens), BF16),
             pltpu.VMEM((n, HD, tokens), F32),

time: 104 us -> 103 us (level)
  no operation moved by 1% of the time
where the time goes in v5:
time: 103 us
  Pallas kernels  98.5 us (96%)
  local copies, waits for them, and re-layouts  3.32 us (3%)
  between operations  1.29 us (1%)
    pallas_call x1, Pallas kernels, run_step(): pl.pallas_call(functools.partial(step_kernel, n_wide, n), out_shape=(pltp...  98.5 us
    unnamed x3, local copies, waits for them, and re-layouts  3.32 us

profile of v5, /device:TPU:1, one launch (start us, length us, event | category | flops | bytes accessed | tf_op | source)
XLA Modules:
  0.0 103.1 jit_solution(4238936225337226106)
XLA Ops:
  1.3 98.5 %shard_map.94 = (bf16[256,512]{1,0:T(8,128)(2,1)S(1)}, f32[2048,512]{1,0:T(8,128)S(1)}, f32[16,128]{1,0:T(8,128)S(1)}) custom-call(f32[2048,512]{1,0:T(8,128)} %table_ref.1, f32[16,128]{1,0:T(8,128)} %bitcast.7, s32[1,256]{1,0:T(1,128)} %ids_ref.1, s32[1]{0:T(128)S(6)} %copy.16.len_ref, bf16[512,2048]{1,0:T(8,128)(2,1)} %w_hbm.1, bf16[512,512]{1,0:T(8,128)(2,1)} %wo_hbm.1, ...), custom_call_target="tpu_custom_call" | custom-call | tf_op jit(solution)/shard_map/pallas_call | solution.py:511
  99.8 0.7 copy.13
  100.5 0.6 copy.15
  101.1 2.0 %copy.14 = f32[2048,512]{1,0:T(8,128)} copy(f32[2048,512]{1,0:T(8,128)S(1)} %get-tuple-element.10) | data formatting | bytes 8388608

commit v6 on v5

--- a/solution.py
+++ b/solution.py
@@ -401,6 +401,9 @@
                     give_sem.at[1],
                     {"wide": o, "narrow": y * 2 + core},
                 ).start()
+    for wait in finish:
+        wait()
+    finish.clear()
     finish.append(lambda: wait_bytes(outgoing.at[pl.ds(0, chips * slots - CAP)], give_sem.at[0]))
     arriving[own, :] = outgoing[own, :]
     wait_bytes(arriving.at[pl.ds(0, chips * slots - CAP)], give_sem.at[1])

time: 103 us -> 103 us (level)
  no operation moved by 1% of the time
where the time goes in v6:
time: 103 us
  Pallas kernels  98 us (95%)
  local copies, waits for them, and re-layouts  3.32 us (3%)
  between operations  1.29 us (1%)
    pallas_call x1, Pallas kernels, run_step(): pl.pallas_call(functools.partial(step_kernel, n_wide, n), out_shape=(pltp...  98 us
    unnamed x3, local copies, waits for them, and re-layouts  3.32 us

profile of v6, /device:TPU:1, one launch (start us, length us, event | category | flops | bytes accessed | tf_op | source)
XLA Modules:
  0.0 102.6 jit_solution(1602147411668792360)
XLA Ops:
  1.3 98.0 %shard_map.94 = (bf16[256,512]{1,0:T(8,128)(2,1)S(1)}, f32[2048,512]{1,0:T(8,128)S(1)}, f32[16,128]{1,0:T(8,128)S(1)}) custom-call(f32[2048,512]{1,0:T(8,128)} %table_ref.1, f32[16,128]{1,0:T(8,128)} %bitcast.7, s32[1,256]{1,0:T(1,128)} %ids_ref.1, s32[1]{0:T(128)S(6)} %copy.16.len_ref, bf16[512,2048]{1,0:T(8,128)(2,1)} %w_hbm.1, bf16[512,512]{1,0:T(8,128)(2,1)} %wo_hbm.1, ...), custom_call_target="tpu_custom_call" | custom-call | tf_op jit(solution)/shard_map/pallas_call | solution.py:514
  99.3 0.7 copy.13
  100.0 0.6 copy.15
  100.6 2.0 %copy.14 = f32[2048,512]{1,0:T(8,128)} copy(f32[2048,512]{1,0:T(8,128)S(1)} %get-tuple-element.10) | data formatting | bytes 8388608
